TPU v7x, 256 devices: a whole 4x4x8 slice. The times are simulated.
256 devices in a mesh: outer: 64 (over x_hi, z, y), inner: 4 (over x_lo, core).
Axes of the slice: x: 4 (x_hi: 2, x_lo: 2; x = x_hi * 2 + x_lo), y: 4, z: 8, core: 2. Of those that a mesh axis runs over, the one named last changes fastest.
Arguments:
- tokens: bfloat16 [32768, 2560], P(('outer', 'inner')), may hold values from -6 to 6
- norm_gain: float32 [2560], replicated, may hold values from 0.1 to 1.9
- w_query: bfloat16 [2560, 2560], P(None, 'inner'), may hold values from -0.15625 to 0.15625
- b_query: float32 [2560], P('inner'), may hold values from -24 to 24
- w_key: bfloat16 [2560, 512], P(None, 'inner'), may hold values from -0.25 to 0.25
- b_key: float32 [512], P('inner'), may hold values from -40 to 40
- w_value: bfloat16 [2560, 512], P(None, 'inner'), may hold values from -0.125 to 0.125
- b_value: float32 [512], P('inner'), may hold values from -3 to 3
- w_out: bfloat16 [2560, 2560], P('inner'), may hold values from -0.125 to 0.125
- positions: int32 [32768], P(('outer', 'inner')), may hold values from 0 to 32767, as said below
Outputs:
- attended: bfloat16 [32768, 2560], P(('outer', 'inner'))
Inputs may be any that keep to these rules, and one draw needn't show every extreme that they name: Block b holds two whole runs of 256 consecutive positions in order: run c in its first half and run 2 * 64 - 1 - c in its second, where c differs from block to block; every position occurs once.
All inputs are finite; a program needn't handle non-finite values.
Results may differ from a plain program's by a relative error of at most 0.017.
The roundings to bfloat16 on the way count: a program that leaves them out, or rounds other values in their place, can miss the bound.
Values may be sent and summed in bfloat16 or wider, within the bound.
No kernel may reach another device: no remote copies, remote signals or barrier semaphores. Data moves between devices by JAX's collectives and lax.ppermute only.
A program may use at most 64 MiB of HBM per device.

v0:
```python
import functools

import jax
import jax.numpy as jnp
from jax import lax
from jax.experimental import pallas as pl
from jax.experimental.pallas import tpu as pltpu
from jax.sharding import PartitionSpec as P

HEAD_DIM = 128
VISITS = 14
HALF = 256
SHARD = 128
STRIP = 128
HEADS = 5
TILE = 16
MSG = HALF + HALF + TILE
STATE = HEAD_DIM + 16
PEAK, TOTAL = HEAD_DIM, HEAD_DIM + 8

rope_base = 10000000.0
norm_eps = 1e-06
masked_score = -1e30
EXP_SCALE = HEAD_DIM ** (-0.5) * 1.4426950408889634
F32, BF16 = jnp.float32, jnp.bfloat16
VMEM_BYTES = 24 * 2**20

WHOLE = pl.BlockSpec(memory_space=pltpu.VMEM)
SCALARS = pl.BlockSpec(memory_space=pltpu.SMEM)


def params():
    return pltpu.CompilerParams(vmem_limit_bytes=VMEM_BYTES)


def cost(flops, data, exps=0):
    return pl.CostEstimate(flops=flops, bytes_accessed=data, transcendentals=exps)


def where_am_i(pos_ref, runs):
    first = pos_ref[0]
    run = lax.shift_right_logical(first, 8)
    second = run >= runs // 2
    lead = jnp.where(second, runs - 1 - run, run)
    core = lax.bitwise_and(lax.shift_right_logical(first, 7), 1)
    return lead, jnp.where(second, 1, 0), core


def norm_kernel(tokens_ref, gain_ref, out_ref):
    values = tokens_ref[...].astype(F32)
    scale = lax.rsqrt(jnp.mean(values * values, axis=-1, keepdims=True) + norm_eps)
    out_ref[...] = (values * scale * gain_ref[...][None, :]).astype(BF16)


def normalize(tokens, gain):
    return pl.pallas_call(
        norm_kernel,
        out_shape=jax.ShapeDtypeStruct(tokens.shape, BF16),
        in_specs=[WHOLE, WHOLE],
        out_specs=WHOLE,
        compiler_params=params(),
        cost_estimate=cost(5 * tokens.size, 4 * tokens.size),
    )(tokens, gain)


def gather_rows(pos_ref, runs, own_ref, other_ref, rows):
    lead, _, core = where_am_i(pos_ref, runs)
    rows[pl.ds(pl.multiple_of(core * SHARD, SHARD), SHARD), :] = own_ref[...]
    rows[pl.ds(pl.multiple_of((1 - core) * SHARD, SHARD), SHARD), :] = other_ref[...]
    return lead


def rope_for(half, cos_ref, sin_ref):
    lane = lax.broadcasted_iota(jnp.int32, (HALF, HEAD_DIM), 1)
    mine = (lane < HEAD_DIM // 2) if half == 0 else (lane >= HEAD_DIM // 2)
    cos, sin = cos_ref[...], sin_ref[...]
    cos = jnp.where(mine, cos, pltpu.roll(cos, HEAD_DIM // 2, 1))
    sin = jnp.where(mine, sin, pltpu.roll(sin, HEAD_DIM // 2, 1))
    sin = jnp.where(lane < HEAD_DIM // 2, -sin, sin)
    return lambda u: u * cos + pltpu.roll(u, HEAD_DIM // 2, 1) * sin


def key_kernel(half, runs, pos_ref, own_ref, other_ref, wk_ref, wv_ref, bk_ref, bv_ref, cos_ref, sin_ref,
               msg_ref, rows):
    lead = gather_rows(pos_ref, runs, own_ref, other_ref, rows)
    x = rows[...]
    rope = rope_for(half, cos_ref, sin_ref)
    keys = jnp.dot(x, wk_ref[...], preferred_element_type=F32) + bk_ref[...][None, :]
    msg_ref[0:HALF, :] = rope(keys).astype(BF16)
    values = jnp.dot(x, wv_ref[...], preferred_element_type=F32) + bv_ref[...][None, :]
    flipped = values.T.astype(BF16)
    msg_ref[HALF:HALF + SHARD, :] = flipped[:, 0:SHARD]
    msg_ref[HALF + SHARD:2 * HALF, :] = flipped[:, SHARD:HALF]
    msg_ref[2 * HALF:MSG, :] = jnp.full((TILE, HEAD_DIM), lead.astype(F32), F32).astype(BF16)


def query_kernel(half, runs, pos_ref, own_ref, other_ref, wq_ref, bq_ref, cos_ref, sin_ref, q_ref, rows):
    gather_rows(pos_ref, runs, own_ref, other_ref, rows)
    x = rows[...]
    rope = rope_for(half, cos_ref, sin_ref)
    for h in range(HEADS):
        cols = slice(h * HEAD_DIM, (h + 1) * HEAD_DIM)
        heads = jnp.dot(x, wq_ref[:, cols], preferred_element_type=F32) + bq_ref[cols][None, :]
        q_ref[:, h * HALF:(h + 1) * HALF] = rope(heads).T.astype(BF16)


def project_keys(half, runs, positions, own, other, weights, cos, sin):
    features = own.shape[1]
    return pl.pallas_call(
        functools.partial(key_kernel, half, runs),
        out_shape=jax.ShapeDtypeStruct((MSG, HEAD_DIM), BF16),
        in_specs=[SCALARS] + [WHOLE] * 8,
        out_specs=WHOLE,
        scratch_shapes=[pltpu.VMEM((HALF, features), BF16)],
        compiler_params=params(),
        cost_estimate=cost(4 * HALF * features * HEAD_DIM, 4 * features * HEAD_DIM),
    )(positions, own, other, *weights, cos, sin)


def project_queries(half, runs, positions, own, other, w_query, b_query, cos, sin):
    features = own.shape[1]
    return pl.pallas_call(
        functools.partial(query_kernel, half, runs),
        out_shape=jax.ShapeDtypeStruct((HEAD_DIM, HEADS * HALF), BF16),
        in_specs=[SCALARS] + [WHOLE] * 6,
        out_specs=WHOLE,
        scratch_shapes=[pltpu.VMEM((HALF, features), BF16)],
        compiler_params=params(),
        cost_estimate=cost(2 * HALF * features * HEADS * HEAD_DIM, 2 * features * HEADS * HEAD_DIM),
    )(positions, own, other, w_query, b_query, cos, sin)


def distance(kind, level, column):
    if kind == "up":
        return 4 * level + 0 * column
    if kind == "even":
        return 4 * level + column - lax.bitwise_xor(column, 1)
    if kind == "odd":
        return 4 * level + 2 * column - 3
    if kind == "cross":
        return 4 * level + jnp.where(column < 2, -2, 2)
    return jnp.where(column == 0, VISITS - 1, 0)


def visit(q_ref, msgs, state, at, first=False):
    k = msgs[at, 0:HALF, :]
    vt = jnp.concatenate([msgs[at, HALF:HALF + SHARD, :], msgs[at, HALF + SHARD:2 * HALF, :]], axis=1)
    for strip in range(HEADS * HALF // STRIP):
        cols = slice(strip * STRIP, (strip + 1) * STRIP)
        s = jnp.dot(k, q_ref[:, cols], preferred_element_type=F32)
        if first:
            key_at = lax.broadcasted_iota(jnp.int32, s.shape, 0)
            row_at = lax.broadcasted_iota(jnp.int32, s.shape, 1) + strip * STRIP % HALF
            s = jnp.where(key_at <= row_at, s, masked_score)
            peak = jnp.max(s, axis=0, keepdims=True)
        else:
            old = state[PEAK:PEAK + 1, cols]
            peak = jnp.maximum(old, jnp.max(s, axis=0, keepdims=True))
            factor = jnp.exp2((old - peak) * EXP_SCALE)
        expo = jnp.exp2((s - peak) * EXP_SCALE)
        total = jnp.sum(expo, axis=0, keepdims=True)
        mixed = jnp.dot(vt, expo.astype(BF16), preferred_element_type=F32)
        if not first:
            total = total + state[TOTAL:TOTAL + 1, cols] * factor
            mixed = mixed + state[0:HEAD_DIM, cols] * factor
        state[PEAK:PEAK + 1, cols] = peak
        state[TOTAL:TOTAL + 1, cols] = total
        state[0:HEAD_DIM, cols] = mixed


def attend_all(target, specs, places, arrays, pos_ref, runs, q_ref, msgs, state, todo, own=(), paired=False):
    lead, second, _ = where_am_i(pos_ref, runs)
    column = lax.bitwise_and(pos_ref[SHARD], 3)
    todo[0] = 0
    wanted = []
    for (half, kind, level), (which, index) in zip(specs, places):
        back = distance(kind, level, column)
        valid = jnp.logical_and(back >= 1, back <= VISITS - 1)
        role = second if half == 0 else 1 - second
        if half == target:
            run = jnp.max(arrays[which][index, 2 * HALF:MSG, :].astype(F32)).astype(jnp.int32)
            seen = jnp.where(role == 0, run < lead, run > lead)
        else:
            seen = role == 0
        wanted.append(jnp.logical_and(valid, seen))
    sources = [(arrays[which], index) for which, index in places]
    if own:
        msgs[0, :, :] = own[target][0, :, :]
        visit(q_ref, msgs, state, 0, True)
        wanted.append(second == 1 - target)
        sources.append((own[1 - target], 0))
    for want, (ref, index) in zip(wanted, sources):
        @pl.when(want)
        def _(ref=ref, index=index):
            place = todo[0]
            msgs[place, :, :] = ref[index, :, :]
            todo[0] = place + 1

    count = todo[0]

    def one(i, carry):
        visit(q_ref, msgs, state, i)
        return carry

    def two(i, carry):
        visit(q_ref, msgs, state, 2 * i)
        visit(q_ref, msgs, state, 2 * i + 1)
        return carry

    if paired:
        lax.fori_loop(0, lax.shift_right_logical(count, 1), two, 0)

        @pl.when(lax.bitwise_and(count, 1) == 1)
        def _():
            visit(q_ref, msgs, state, count - 1)
    else:
        lax.fori_loop(0, count, one, 0)


def attend_kernel(target, specs, places, own, runs, pos_ref, q_ref, *rest):
    state, msgs, todo = rest[-3:]
    if own:
        attend_all(target, specs, places, rest[2:-3], pos_ref, runs, q_ref, msgs, state, todo, own=rest[:2])
    else:
        state[...] = rest[0][...]
        attend_all(target, specs, places, rest[1:-3], pos_ref, runs, q_ref, msgs, state, todo)


def unpack(messages):
    arrays, places, specs = [], [], []
    for half, kind, level, array, at in messages:
        for i, known in enumerate(arrays):
            if known is array:
                break
        else:
            i = len(arrays)
            arrays.append(array)
        places.append((i, at))
        specs.append((half, kind, level))
    return tuple(specs), tuple(places), arrays


def working(count):
    return [pltpu.VMEM((count, MSG, HEAD_DIM), BF16), pltpu.SMEM((1,), jnp.int32)]


def task_cost(count, more=0):
    return cost(count * 2 * HEADS * HALF * HALF * HEAD_DIM + more, 2**21, count * HEADS * HALF * HALF // 2)


def attend(target, messages, runs, positions, q, state=None, own=()):
    specs, places, arrays = unpack(messages)
    before = list(own) if own else [state]
    return pl.pallas_call(
        functools.partial(attend_kernel, target, specs, places, bool(own), runs),
        out_shape=jax.ShapeDtypeStruct((STATE, HEADS * HALF), F32),
        in_specs=[SCALARS] + [WHOLE] * (1 + len(before) + len(arrays)),
        out_specs=WHOLE,
        scratch_shapes=working(len(specs) + 1),
        compiler_params=params(),
        cost_estimate=task_cost(len(specs)),
    )(positions, q, *before, *arrays)


def project_out(pos_ref, runs, mixed, w_ref, keep_ref, send_ref):
    _, _, core = where_am_i(pos_ref, runs)
    keep_at = pl.ds(pl.multiple_of(core * SHARD, SHARD), SHARD)
    send_at = pl.ds(pl.multiple_of((1 - core) * SHARD, SHARD), SHARD)
    x = jnp.concatenate([mixed[send_at, :], mixed[keep_at, :]], axis=0)
    width = 512
    for j in range(w_ref.shape[1] // width):
        cols = slice(j * width, (j + 1) * width)
        part = jnp.dot(x, w_ref[:, cols], preferred_element_type=F32).astype(BF16)
        send_ref[:, cols] = part[0:SHARD]
        keep_ref[:, cols] = part[SHARD:HALF]


def last_kernel(target, specs, places, runs, pos_ref, q_ref, state_in, w_ref, *rest):
    keep_ref, send_ref, msgs, todo, state, mixed = rest[-6:]
    state[...] = state_in[...]
    attend_all(target, specs, places, rest[:-6], pos_ref, runs, q_ref, msgs, state, todo, paired=target == 0)
    for h in range(HEADS):
        cols = slice(h * HALF, (h + 1) * HALF)
        scale = 1.0 / state[TOTAL:TOTAL + 1, cols]
        mixed[:, h * HEAD_DIM:(h + 1) * HEAD_DIM] = (state[0:HEAD_DIM, cols] * scale).T.astype(BF16)
    project_out(pos_ref, runs, mixed, w_ref, keep_ref, send_ref)


def attend_last(target, messages, runs, positions, q, state, w_out):
    specs, places, arrays = unpack(messages)
    part = jax.ShapeDtypeStruct((SHARD, w_out.shape[1]), BF16)
    return pl.pallas_call(
        functools.partial(last_kernel, target, specs, places, runs),
        out_shape=(part, part),
        in_specs=[SCALARS] + [WHOLE] * (3 + len(arrays)),
        out_specs=(WHOLE, WHOLE),
        scratch_shapes=working(len(specs)) + [pltpu.VMEM(state.shape, F32), pltpu.VMEM((HALF, HEADS * HEAD_DIM), BF16)],
        compiler_params=params(),
        cost_estimate=task_cost(len(specs), 2 * HALF * w_out.size),
    )(positions, q, state, w_out, *arrays)


def after(x, *earlier):
    return lax.optimization_barrier((x, *earlier))[0]


def local(tokens, norm_gain, w_query, b_query, w_key, b_key, w_value, b_value, w_out, positions):
    outer = lax.axis_size("outer")
    runs = 2 * outer

    def along(x, distance):
        return lax.ppermute(x, "outer", [(i, (i + distance) % outer) for i in range(outer)])

    def across(x, flip):
        return lax.ppermute(x, "inner", [(i, i ^ flip) for i in range(4)])

    far_tokens = across(tokens, 2)
    normed = normalize(tokens, norm_gain)
    near = across(normed, 1)

    run = positions[0] // HALF
    positions = jnp.concatenate([positions, lax.axis_index("outer")[None]])
    row = jnp.arange(HALF, dtype=jnp.int32)[:, None]
    lane = jnp.arange(HEAD_DIM, dtype=jnp.int32)[None, :]
    places = jnp.where(lane < HEAD_DIM // 2, run, runs - 1 - run) * HALF + row
    inverse = rope_base ** (-(jnp.arange(HEAD_DIM // 2, dtype=F32) * 2.0 / HEAD_DIM))
    angles = places.astype(F32) * jnp.concatenate([inverse, inverse])[None, :]
    cos, sin = jnp.cos(angles), jnp.sin(angles)

    kv = (w_key, w_value, b_key, b_value)
    ring = range(outer)

    def pack(*parts):
        return jnp.concatenate(parts, axis=0)

    def up(x):
        return along(x, 4)

    def even(x):
        return lax.ppermute(x, "outer", [(i, i ^ 1) for i in ring])

    def odd(x):
        return lax.ppermute(x, "outer", [(i, i ^ 3) for i in ring])

    def corner(x):
        return lax.ppermute(x, "outer", [(i, (i + 7 - 2 * (i % 4)) % outer) for i in ring if i % 4 >= 2])

    A, B = 0, 1

    a0 = project_keys(0, runs, positions, normed, near, kv, cos, sin)[None]
    a1, e0, o0 = up(a0), even(a0), odd(a0)
    qa = project_queries(0, runs, positions, after(normed, a0), near, w_query, b_query, cos, sin)

    far_tokens = after(far_tokens, qa, a1, e0, o0)
    far_near = normalize(across(far_tokens, 1), norm_gain)
    far = normalize(far_tokens, norm_gain)
    b0 = project_keys(1, runs, positions, far, far_near, kv, cos, sin)[None]
    u0 = pack(a1, b0)
    u1, e1, o1 = up(u0), even(pack(u0, o0)), odd(u0)
    qb = project_queries(1, runs, positions, after(far, b0), far_near, w_query, b_query, cos, sin)
    came1 = ((A, "up", 1, a1, 0), (A, "even", 0, e0, 0), (A, "odd", 0, o0, 0))
    state = attend(B, came1, runs, positions, qb, own=(a0, b0))

    v1 = after(u1, state)
    u2, e2, o2 = up(v1), even(pack(v1, o1[1:2])), odd(pack(v1, e1[0:1]))
    came2 = ((A, "up", 2, u1, 0), (B, "up", 1, u1, 1), (A, "even", 1, e1, 0), (B, "even", 0, e1, 1),
             (A, "cross", 0, e1, 2), (A, "odd", 1, o1, 0), (B, "odd", 0, o1, 1))
    state = attend(B, came2, runs, positions, qb, state)
    near_state = attend(A, came1, runs, positions, after(qa, state), own=(a0, b0))

    v2 = after(u2, near_state)
    u3, e3, o3 = up(pack(v2[1:2], o2[2:3])), even(pack(v2, o2[1:2])), odd(v2)
    came3 = ((A, "up", 3, u2, 0), (B, "up", 2, u2, 1), (A, "even", 2, e2, 0), (B, "even", 1, e2, 1),
             (B, "cross", 0, e2, 2), (A, "odd", 2, o2, 0), (B, "odd", 1, o2, 1), (A, "cross", 1, o2, 2))
    state = attend(B, came3, runs, positions, qb, state)

    v3 = after(u3, state)
    u4, e4, o4 = up(pack(v3[1:2], o3[0:1])), even(pack(v3[0:1], o3[1:2])), odd(v3[0:1])
    c4 = corner(pack(v3[0:1], e3[1:2]))
    came4 = ((B, "up", 3, u3, 0), (A, "cross", 2, u3, 1), (A, "even", 3, e3, 0), (B, "even", 2, e3, 1),
             (B, "cross", 1, e3, 2), (A, "odd", 3, o3, 0), (B, "odd", 2, o3, 1))
    state = attend(B, came4, runs, positions, qb, state)
    near_state = attend(A, came2, runs, positions, after(qa, state), near_state)
    came5 = ((B, "even", 3, e4, 0), (B, "cross", 2, e4, 1), (B, "odd", 3, o4, 0), (A, "cross", 3, u4, 0),
             (A, "corner", 3, u4, 1), (B, "corner", 3, c4, 0), (B, "cross", 3, c4, 1))

    keep_far, send_far = attend_last(B, came5, runs, positions, after(qb, near_state), state, w_out)
    got_far = across(send_far, 1)
    other = (keep_far.astype(F32) + got_far.astype(F32)).astype(BF16)
    arrived = across(other, 2)
    keep_near, send_near = attend_last(
        A, came3 + came4 + came5, runs, positions, after(qa, other), near_state, w_out
    )
    got_near = across(send_near, 1)
    return (keep_near.astype(F32) + got_near.astype(F32) + arrived.astype(F32)).astype(BF16)


def solution(mesh):
    in_specs = (
        P(("outer", "inner"), None),
        P(),
        P(None, "inner"),
        P("inner"),
        P(None, "inner"),
        P("inner"),
        P(None, "inner"),
        P("inner"),
        P("inner", None),
        P(("outer", "inner")),
    )
    out_specs = P(("outer", "inner"), None)
    return jax.shard_map(local, mesh=mesh, in_specs=in_specs, out_specs=out_specs, check_vma=False)
```

profile of v0, /device:TPU:1, one launch (start us, length us, event | category | flops | bytes accessed | tf_op | source)
XLA Modules:
  0.0 104.7 jit_solution(3255728616537432153)
XLA Ops:
  0.0 2.0 %collective-permute-start.1 = (bf16[128,2560]{1,0:T(8,128)(2,1)}, bf16[128,2560]{1,0:T(8,128)(2,1)S(1)}, u32[]{:S(2)}, u32[]{:S(2)}) collective-permute-start(bf16[128,2560]{1,0:T(8,128)(2,1)} %tokens_ref.1), channel_id=1, source_target_pairs={{0,2},{1,3},{2,0},{3,1},{4,6},{5,7},{6,4},{7,5},{8,10},{9,11},{10,... | collective-permute-start | bytes 1966088 | tf_op jit(solution)/shard_map/ppermute | solution.py:315
  4.2 1.4 %collective-permute-start = (bf16[128,2560]{1,0:T(8,128)(2,1)S(1)}, bf16[128,2560]{1,0:T(8,128)(2,1)S(1)}, u32[]{:S(2)}, u32[]{:S(2)}) collective-permute-start(bf16[128,2560]{1,0:T(8,128)(2,1)S(1)} %shard_map.100.own_ref), channel_id=1, source_target_pairs={{0,1},{1,0},{2,3},{3,2},{4,5},{5,4},{6,7},{7,6},{8,9},{9,8},{10,11... | collective-permute-start | bytes 1966088 | tf_op jit(solution)/shard_map/ppermute | solution.py:315
  7.3 1.5 %shard_map.101 = bf16[528,128]{1,0:T(8,128)(2,1)S(1)} custom-call(s32[129]{0:T(256)S(1)} %pad_add_fusion.pos_ref, bf16[128,2560]{1,0:T(8,128)(2,1)S(1)} %shard_map.100.own_ref, bf16[128,2560]{1,0:T(8,128)(2,1)S(1)} %collective-permute-done.other_ref, bf16[2560,128]{1,0:T(8,128)(2,1)S(1)} %copy-done.2, bf16[2560,128]{1,0:T(8,128)(2,1)S(1)} %copy-done.3, ...), custom_call_target="tpu_custom_call" | custom-call | flops 335544320 | bytes 1310720 | tf_op jit(solution)/shard_map/pallas_call | solution.py:109
  8.9 1.4 %collective-permute-start.2 = (bf16[1,528,128]{2,1,0:T(8,128)(2,1)S(1)}, bf16[1,528,128]{2,1,0:T(8,128)(2,1)S(1)}, u32[]{:S(2)}, u32[]{:S(2)}) collective-permute-start(bf16[1,528,128]{2,1,0:T(8,128)(2,1)S(1)} %bitcast.9), channel_id=1, source_target_pairs={{0,16},{4,20},{8,24},{12,28},{16,32},{20,36},{24,40},{28,44},{32,4... | collective-permute-start | bytes 405512 | tf_op jit(solution)/shard_map/ppermute | solution.py:312
  10.3 1.3 %collective-permute-start.3 = (bf16[1,528,128]{2,1,0:T(8,128)(2,1)S(1)}, bf16[1,528,128]{2,1,0:T(8,128)(2,1)S(1)}, u32[]{:S(2)}, u32[]{:S(2)}) collective-permute-start(bf16[1,528,128]{2,1,0:T(8,128)(2,1)S(1)} %bitcast.10), channel_id=1, source_target_pairs={{0,4},{4,0},{8,12},{12,8},{16,20},{20,16},{24,28},{28,24},{32,36},... | collective-permute-start | bytes 405512 | tf_op jit(solution)/shard_map/ppermute | solution.py:340
  11.6 1.9 %collective-permute-start.4 = (bf16[1,528,128]{2,1,0:T(8,128)(2,1)S(1)}, bf16[1,528,128]{2,1,0:T(8,128)(2,1)S(1)}, u32[]{:S(2)}, u32[]{:S(2)}) collective-permute-start(bf16[1,528,128]{2,1,0:T(8,128)(2,1)S(1)} %bitcast.11), channel_id=1, source_target_pairs={{0,12},{4,8},{8,4},{12,0},{16,28},{20,24},{24,20},{28,16},{32,44},... | collective-permute-start | bytes 405512 | tf_op jit(solution)/shard_map/ppermute | solution.py:343
  13.5 2.7 %shard_map.102.q_ref = bf16[128,1280]{1,0:T(8,128)(2,1)S(1)} custom-call(s32[129]{0:T(256)S(1)} %pad_add_fusion.pos_ref, bf16[128,2560]{1,0:T(8,128)(2,1)S(1)} %shard_map.100.own_ref, bf16[128,2560]{1,0:T(8,128)(2,1)S(1)} %collective-permute-done.other_ref, bf16[2560,640]{1,0:T(8,128)(2,1)S(1)} %copy-done, f32[640]{0:T(1024)S(1)} %copy-done.7, ...), custom_call_target="tpu_custom_call" | custom-call | flops 838860800 | bytes 3276800 | tf_op jit(solution)/shard_map/pallas_call | solution.py:122
  16.2 2.2 %collective-permute-done.1.tokens_ref = bf16[128,2560]{1,0:T(8,128)(2,1)S(1)} collective-permute-done((bf16[128,2560]{1,0:T(8,128)(2,1)}, bf16[128,2560]{1,0:T(8,128)(2,1)S(1)}, u32[]{:S(2)}, u32[]{:S(2)}) %collective-permute-start.1) | collective-permute-done | bytes 655392 | tf_op jit(solution)/shard_map/ppermute | solution.py:315
  18.4 1.7 %collective-permute-done.2.rest_2_ = bf16[1,528,128]{2,1,0:T(8,128)(2,1)S(1)} collective-permute-done((bf16[1,528,128]{2,1,0:T(8,128)(2,1)S(1)}, bf16[1,528,128]{2,1,0:T(8,128)(2,1)S(1)}, u32[]{:S(2)}, u32[]{:S(2)}) %collective-permute-start.2) | collective-permute-done | bytes 135200 | tf_op jit(solution)/shard_map/ppermute | solution.py:312
  21.4 1.4 %collective-permute-done.5.tokens_ref = bf16[128,2560]{1,0:T(8,128)(2,1)S(1)} collective-permute-done((bf16[128,2560]{1,0:T(8,128)(2,1)S(1)}, bf16[128,2560]{1,0:T(8,128)(2,1)S(1)}, u32[]{:S(2)}, u32[]{:S(2)}) %collective-permute-start.5) | collective-permute-done | bytes 655392 | tf_op jit(solution)/shard_map/ppermute | solution.py:315
  23.1 1.5 %shard_map.105 = bf16[528,128]{1,0:T(8,128)(2,1)S(1)} custom-call(s32[129]{0:T(256)S(1)} %pad_add_fusion.pos_ref, bf16[128,2560]{1,0:T(8,128)(2,1)S(1)} %shard_map.103.own_ref, bf16[128,2560]{1,0:T(8,128)(2,1)S(1)} %shard_map.104.other_ref, bf16[2560,128]{1,0:T(8,128)(2,1)S(1)} %copy-done.2, bf16[2560,128]{1,0:T(8,128)(2,1)S(1)} %copy-done.3, ...), custom_call_target="tpu_custom_call" | custom-call | flops 335544320 | bytes 1310720 | tf_op jit(solution)/shard_map/pallas_call | solution.py:109
  24.7 1.5 %collective-permute-start.7 = (bf16[3,528,128]{2,1,0:T(8,128)(2,1)S(1)}, bf16[3,528,128]{2,1,0:T(8,128)(2,1)S(1)}, u32[]{:S(2)}, u32[]{:S(2)}) collective-permute-start(bf16[3,528,128]{2,1,0:T(8,128)(2,1)S(1)} %pad_maximum_fusion.2), channel_id=1, source_target_pairs={{0,4},{4,0},{8,12},{12,8},{16,20},{20,16},{24,28},{28,24},{32,36},... | collective-permute-start | bytes 1216520 | tf_op jit(solution)/shard_map/ppermute | solution.py:340
  26.4 2.2 %collective-permute-start.8 = (bf16[2,528,128]{2,1,0:T(8,128)(2,1)S(1)}, bf16[2,528,128]{2,1,0:T(8,128)(2,1)S(1)}, u32[]{:S(2)}, u32[]{:S(2)}) collective-permute-start(bf16[2,528,128]{2,1,0:T(8,128)(2,1)S(1)} %pad_maximum_fusion.6), channel_id=1, source_target_pairs={{0,12},{4,8},{8,4},{12,0},{16,28},{20,24},{24,20},{28,16},{32,44},... | collective-permute-start | bytes 811016 | tf_op jit(solution)/shard_map/ppermute | solution.py:343
  28.5 2.7 %shard_map.106.q_ref = bf16[128,1280]{1,0:T(8,128)(2,1)S(1)} custom-call(s32[129]{0:T(256)S(1)} %pad_add_fusion.pos_ref, bf16[128,2560]{1,0:T(8,128)(2,1)S(1)} %shard_map.103.own_ref, bf16[128,2560]{1,0:T(8,128)(2,1)S(1)} %shard_map.104.other_ref, bf16[2560,640]{1,0:T(8,128)(2,1)S(1)} %copy-done, f32[640]{0:T(1024)S(1)} %copy-done.7, ...), custom_call_target="tpu_custom_call" | custom-call | flops 838860800 | bytes 3276800 | tf_op jit(solution)/shard_map/pallas_call | solution.py:122
  31.2 2.7 %shard_map.107.rest_0_ = f32[144,1280]{1,0:T(8,128)S(1)} custom-call(s32[129]{0:T(256)S(1)} %pad_add_fusion.pos_ref, bf16[128,1280]{1,0:T(8,128)(2,1)S(1)} %shard_map.106.q_ref, bf16[1,528,128]{2,1,0:T(8,128)(2,1)S(1)} %bitcast.12, bf16[1,528,128]{2,1,0:T(8,128)(2,1)S(1)} %bitcast.7, bf16[1,528,128]{2,1,0:T(8,128)(2,1)S(1)} %collective-permute-done.2.rest_2_, ...), custom_call_target="tpu_custom_call" | custom-call | flops 251658240 | bytes 2097152 | tf_op jit(solution)/shard_map/pallas_call | solution.py:254
  33.9 3.6 %collective-permute-done.6.rest_1_ = bf16[2,528,128]{2,1,0:T(8,128)(2,1)S(1)} collective-permute-done((bf16[2,528,128]{2,1,0:T(8,128)(2,1)S(1)}, bf16[2,528,128]{2,1,0:T(8,128)(2,1)S(1)}, u32[]{:S(2)}, u32[]{:S(2)}) %collective-permute-start.6) | collective-permute-done | bytes 270368 | tf_op jit(solution)/shard_map/ppermute | solution.py:312
  37.6 2.0 %collective-permute-start.11 = (bf16[3,528,128]{2,1,0:T(8,128)(2,1)S(1)}, bf16[3,528,128]{2,1,0:T(8,128)(2,1)S(1)}, u32[]{:S(2)}, u32[]{:S(2)}) collective-permute-start(bf16[3,528,128]{2,1,0:T(8,128)(2,1)S(1)} %get-tuple-element.39), channel_id=1, source_target_pairs={{0,12},{4,8},{8,4},{12,0},{16,28},{20,24},{24,20},{28,16},{32,44},... | collective-permute-start | bytes 1216520 | tf_op jit(solution)/shard_map/ppermute | solution.py:343
  40.0 3.6 %shard_map.108.rest_0_ = f32[144,1280]{1,0:T(8,128)S(1)} custom-call(s32[129]{0:T(256)S(1)} %pad_add_fusion.pos_ref, bf16[128,1280]{1,0:T(8,128)(2,1)S(1)} %shard_map.106.q_ref, f32[144,1280]{1,0:T(8,128)S(1)} %shard_map.107.rest_0_, bf16[2,528,128]{2,1,0:T(8,128)(2,1)S(1)} %collective-permute-done.6.rest_1_, ...), custom_call_target="tpu_custom_call" | custom-call | flops 587202560 | bytes 2097152 | tf_op jit(solution)/shard_map/pallas_call | solution.py:254
  43.6 1.3 %shard_map.110.rest_0_ = f32[144,1280]{1,0:T(8,128)S(1)} custom-call(s32[129]{0:T(256)S(1)} %pad_add_fusion.pos_ref, bf16[128,1280]{1,0:T(8,128)(2,1)S(1)} %shard_map.102.q_ref, bf16[1,528,128]{2,1,0:T(8,128)(2,1)S(1)} %bitcast.13, bf16[1,528,128]{2,1,0:T(8,128)(2,1)S(1)} %bitcast.8, bf16[1,528,128]{2,1,0:T(8,128)(2,1)S(1)} %collective-permute-done.2.rest_2_, ...), custom_call_target="tpu_custom_call" | custom-call | flops 251658240 | bytes 2097152 | tf_op jit(solution)/shard_map/pallas_call | solution.py:254
  44.8 4.6 %collective-permute-done.9.rest_1_.rest_0_ = bf16[2,528,128]{2,1,0:T(8,128)(2,1)S(1)} collective-permute-done((bf16[2,528,128]{2,1,0:T(8,128)(2,1)S(1)}, bf16[2,528,128]{2,1,0:T(8,128)(2,1)S(1)}, u32[]{:S(2)}, u32[]{:S(2)}) %collective-permute-start.9) | collective-permute-done | bytes 270368 | tf_op jit(solution)/shard_map/ppermute | solution.py:312
  50.6 5.5 %collective-permute-done.14.rest_3_.rest_5_ = bf16[2,528,128]{2,1,0:T(8,128)(2,1)S(1)} collective-permute-done((bf16[2,528,128]{2,1,0:T(8,128)(2,1)S(1)}, bf16[2,528,128]{2,1,0:T(8,128)(2,1)S(1)}, u32[]{:S(2)}, u32[]{:S(2)}) %collective-permute-start.14) | collective-permute-done | bytes 270368 | tf_op jit(solution)/shard_map/ppermute | solution.py:343
  56.1 3.6 %shard_map.109.rest_0_ = f32[144,1280]{1,0:T(8,128)S(1)} custom-call(s32[129]{0:T(256)S(1)} %pad_add_fusion.pos_ref, bf16[128,1280]{1,0:T(8,128)(2,1)S(1)} %shard_map.106.q_ref, f32[144,1280]{1,0:T(8,128)S(1)} %shard_map.108.rest_0_, bf16[2,528,128]{2,1,0:T(8,128)(2,1)S(1)} %collective-permute-done.9.rest_1_.rest_0_, ...), custom_call_target="tpu_custom_call" | custom-call | flops 671088640 | bytes 2097152 | tf_op jit(solution)/shard_map/pallas_call | solution.py:254
  60.0 1.3 %collective-permute-start.18 = (bf16[2,528,128]{2,1,0:T(8,128)(2,1)S(1)}, bf16[2,528,128]{2,1,0:T(8,128)(2,1)S(1)}, u32[]{:S(2)}, u32[]{:S(2)}) collective-permute-start(bf16[2,528,128]{2,1,0:T(8,128)(2,1)S(1)} %get-tuple-element.41), channel_id=1, source_target_pairs={{8,20},{12,16},{24,36},{28,32},{40,52},{44,48},{56,68},{60,64},{72... | collective-permute-start | bytes 811016 | tf_op jit(solution)/shard_map/ppermute | solution.py:346
  61.3 4.0 %collective-permute-start.16 = (bf16[1,528,128]{2,1,0:T(8,128)(2,1)S(1)}, bf16[1,528,128]{2,1,0:T(8,128)(2,1)S(1)}, u32[]{:S(2)}, u32[]{:S(2)}) collective-permute-start(bf16[1,528,128]{2,1,0:T(8,128)(2,1)S(1)} %get-tuple-element.36), channel_id=1, source_target_pairs={{0,12},{4,8},{8,4},{12,0},{16,28},{20,24},{24,20},{28,16},{32,44},... | collective-permute-start | bytes 405512 | tf_op jit(solution)/shard_map/ppermute | solution.py:343
  65.3 2.8 %shard_map.111.state_in = f32[144,1280]{1,0:T(8,128)S(1)} custom-call(s32[129]{0:T(256)S(1)} %pad_add_fusion.pos_ref, bf16[128,1280]{1,0:T(8,128)(2,1)S(1)} %shard_map.106.q_ref, f32[144,1280]{1,0:T(8,128)S(1)} %shard_map.109.rest_0_, bf16[2,528,128]{2,1,0:T(8,128)(2,1)S(1)} %collective-permute-done.12.rest_1_.rest_3_, ...), custom_call_target="tpu_custom_call" | custom-call | flops 587202560 | bytes 2097152 | tf_op jit(solution)/shard_map/pallas_call | solution.py:254
  68.1 2.9 %shard_map.112.state_in = f32[144,1280]{1,0:T(8,128)S(1)} custom-call(s32[129]{0:T(256)S(1)} %pad_add_fusion.pos_ref, bf16[128,1280]{1,0:T(8,128)(2,1)S(1)} %shard_map.102.q_ref, f32[144,1280]{1,0:T(8,128)S(1)} %shard_map.110.rest_0_, bf16[2,528,128]{2,1,0:T(8,128)(2,1)S(1)} %collective-permute-done.6.rest_1_, ...), custom_call_target="tpu_custom_call" | custom-call | flops 587202560 | bytes 2097152 | tf_op jit(solution)/shard_map/pallas_call | solution.py:254
  71.0 5.4 %collective-permute-done.18.rest_3_.rest_9_ = bf16[2,528,128]{2,1,0:T(8,128)(2,1)S(1)} collective-permute-done((bf16[2,528,128]{2,1,0:T(8,128)(2,1)S(1)}, bf16[2,528,128]{2,1,0:T(8,128)(2,1)S(1)}, u32[]{:S(2)}, u32[]{:S(2)}) %collective-permute-start.18) | collective-permute-done | bytes 270368 | tf_op jit(solution)/shard_map/ppermute | solution.py:346
  76.5 4.2 %shard_map.113 = (bf16[128,2560]{1,0:T(8,128)(2,1)S(1)}, bf16[128,2560]{1,0:T(8,128)(2,1)S(1)}) custom-call(s32[129]{0:T(256)S(1)} %pad_add_fusion.pos_ref, bf16[128,1280]{1,0:T(8,128)(2,1)S(1)} %shard_map.106.q_ref, f32[144,1280]{1,0:T(8,128)S(1)} %shard_map.111.state_in, bf16[640,2560]{1,0:T(8,128)(2,1)S(1)} %copy-done.1, ...), custom_call_target="tpu_custom_call" | custom-call | flops 1426063360 | bytes 2097152 | tf_op jit(solution)/shard_map/pallas_call | solution.py:292
  80.6 5.1 %collective-permute-start.19 = (bf16[128,2560]{1,0:T(8,128)(2,1)S(1)}, bf16[128,2560]{1,0:T(8,128)(2,1)S(1)}, u32[]{:S(2)}, u32[]{:S(2)}) collective-permute-start(bf16[128,2560]{1,0:T(8,128)(2,1)S(1)} %get-tuple-element.29), channel_id=1, source_target_pairs={{0,1},{1,0},{2,3},{3,2},{4,5},{5,4},{6,7},{7,6},{8,9},{9,8},{10,11... | collective-permute-start | bytes 1966088 | tf_op jit(solution)/shard_map/ppermute | solution.py:315
  85.7 1.7 %collective-permute-done.19 = bf16[128,2560]{1,0:T(8,128)(2,1)S(1)} collective-permute-done((bf16[128,2560]{1,0:T(8,128)(2,1)S(1)}, bf16[128,2560]{1,0:T(8,128)(2,1)S(1)}, u32[]{:S(2)}, u32[]{:S(2)}) %collective-permute-start.19) | collective-permute-done | bytes 655392 | tf_op jit(solution)/shard_map/ppermute | solution.py:315
  87.7 6.6 %shard_map.114 = (bf16[128,2560]{1,0:T(8,128)(2,1)S(1)}, bf16[128,2560]{1,0:T(8,128)(2,1)S(1)}) custom-call(s32[129]{0:T(256)S(1)} %pad_add_fusion.pos_ref, bf16[128,1280]{1,0:T(8,128)(2,1)S(1)} %shard_map.102.q_ref, f32[144,1280]{1,0:T(8,128)S(1)} %shard_map.112.state_in, bf16[640,2560]{1,0:T(8,128)(2,1)S(1)} %copy-done.1, ...), custom_call_target="tpu_custom_call" | custom-call | flops 2684354560 | bytes 2097152 | tf_op jit(solution)/shard_map/pallas_call | solution.py:292
  94.8 8.8 %collective-permute-done.21 = bf16[128,2560]{1,0:T(8,128)(2,1)S(1)} collective-permute-done((bf16[128,2560]{1,0:T(8,128)(2,1)S(1)}, bf16[128,2560]{1,0:T(8,128)(2,1)S(1)}, u32[]{:S(2)}, u32[]{:S(2)}) %collective-permute-start.21) | collective-permute-done | bytes 655392 | tf_op jit(solution)/shard_map/ppermute | solution.py:315
  (70 shorter events, 9.2 us)
Async XLA Ops:
  0.0 7.3 %copy-start.2 = (bf16[2560,128]{1,0:T(8,128)(2,1)S(1)}, bf16[2560,128]{1,0:T(8,128)(2,1)}, u32[]{:S(2)}) copy-start(bf16[2560,128]{1,0:T(8,128)(2,1)} %wk_ref.3) | copy-start | bytes 1966084
  0.0 7.3 %copy-start.3 = (bf16[2560,128]{1,0:T(8,128)(2,1)S(1)}, bf16[2560,128]{1,0:T(8,128)(2,1)}, u32[]{:S(2)}) copy-start(bf16[2560,128]{1,0:T(8,128)(2,1)} %wv_ref.3) | copy-start | bytes 1966084
  0.0 18.4 %collective-permute-start.1 = (bf16[128,2560]{1,0:T(8,128)(2,1)}, bf16[128,2560]{1,0:T(8,128)(2,1)S(1)}, u32[]{:S(2)}, u32[]{:S(2)}) collective-permute-start(bf16[128,2560]{1,0:T(8,128)(2,1)} %tokens_ref.1), channel_id=1, source_target_pairs={{0,2},{1,3},{2,0},{3,1},{4,6},{5,7},{6,4},{7,5},{8,10},{9,11},{10,... | collective-permute-start | bytes 1966088 | tf_op jit(solution)/shard_map/ppermute | solution.py:315
  2.0 1.1 %copy-start.4 = (bf16[128,2560]{1,0:T(8,128)(2,1)S(1)}, bf16[128,2560]{1,0:T(8,128)(2,1)}, u32[]{:S(2)}) copy-start(bf16[128,2560]{1,0:T(8,128)(2,1)} %tokens_ref.1) | copy-start | bytes 1966084
  3.9 1.8 %copy-start.10 = (s32[128]{0:T(128)S(1)}, s32[128]{0:T(128)}, u32[]{:S(2)}) copy-start(s32[128]{0:T(128)} %param.19) | copy-start | bytes 1540
  3.9 3.4 %copy-start.8 = (f32[128]{0:T(128)S(1)}, f32[128]{0:T(128)}, u32[]{:S(2)}) copy-start(f32[128]{0:T(128)} %bk_ref.3) | copy-start | bytes 1540
  3.9 3.4 %copy-start.9 = (f32[128]{0:T(128)S(1)}, f32[128]{0:T(128)}, u32[]{:S(2)}) copy-start(f32[128]{0:T(128)} %bv_ref.3) | copy-start | bytes 1540
  4.2 3.1 %collective-permute-start = (bf16[128,2560]{1,0:T(8,128)(2,1)S(1)}, bf16[128,2560]{1,0:T(8,128)(2,1)S(1)}, u32[]{:S(2)}, u32[]{:S(2)}) collective-permute-start(bf16[128,2560]{1,0:T(8,128)(2,1)S(1)} %shard_map.100.own_ref), channel_id=1, source_target_pairs={{0,1},{1,0},{2,3},{3,2},{4,5},{5,4},{6,7},{7,6},{8,9},{9,8},{10,11... | collective-permute-start | bytes 1966088 | tf_op jit(solution)/shard_map/ppermute | solution.py:315
  5.9 7.6 %copy-start = (bf16[2560,640]{1,0:T(8,128)(2,1)S(1)}, bf16[2560,640]{1,0:T(8,128)(2,1)}, u32[]{:S(2)}) copy-start(bf16[2560,640]{1,0:T(8,128)(2,1)} %wq_ref.3) | copy-start | bytes 9830404
  7.3 6.2 %copy-start.7 = (f32[640]{0:T(1024)S(1)}, f32[640]{0:T(1024)}, u32[]{:S(2)}) copy-start(f32[640]{0:T(1024)} %bq_ref.3) | copy-start | bytes 7684
  8.9 12.2 %copy-start.6 = (f32[2560]{0:T(1024)S(1)}, f32[2560]{0:T(1024)}, u32[]{:S(2)}) copy-start(f32[2560]{0:T(1024)} %gain_ref.5) | copy-start | bytes 30724
  8.9 11.2 %collective-permute-start.2 = (bf16[1,528,128]{2,1,0:T(8,128)(2,1)S(1)}, bf16[1,528,128]{2,1,0:T(8,128)(2,1)S(1)}, u32[]{:S(2)}, u32[]{:S(2)}) collective-permute-start(bf16[1,528,128]{2,1,0:T(8,128)(2,1)S(1)} %bitcast.9), channel_id=1, source_target_pairs={{0,16},{4,20},{8,24},{12,28},{16,32},{20,36},{24,40},{28,44},{32,4... | collective-permute-start | bytes 405512 | tf_op jit(solution)/shard_map/ppermute | solution.py:312
  10.3 9.8 %collective-permute-start.3 = (bf16[1,528,128]{2,1,0:T(8,128)(2,1)S(1)}, bf16[1,528,128]{2,1,0:T(8,128)(2,1)S(1)}, u32[]{:S(2)}, u32[]{:S(2)}) collective-permute-start(bf16[1,528,128]{2,1,0:T(8,128)(2,1)S(1)} %bitcast.10), channel_id=1, source_target_pairs={{0,4},{4,0},{8,12},{12,8},{16,20},{20,16},{24,28},{28,24},{32,36},... | collective-permute-start | bytes 405512 | tf_op jit(solution)/shard_map/ppermute | solution.py:340
  11.6 8.5 %collective-permute-start.4 = (bf16[1,528,128]{2,1,0:T(8,128)(2,1)S(1)}, bf16[1,528,128]{2,1,0:T(8,128)(2,1)S(1)}, u32[]{:S(2)}, u32[]{:S(2)}) collective-permute-start(bf16[1,528,128]{2,1,0:T(8,128)(2,1)S(1)} %bitcast.11), channel_id=1, source_target_pairs={{0,12},{4,8},{8,4},{12,0},{16,28},{20,24},{24,20},{28,16},{32,44},... | collective-permute-start | bytes 405512 | tf_op jit(solution)/shard_map/ppermute | solution.py:343
  20.1 2.7 %collective-permute-start.5 = (bf16[128,2560]{1,0:T(8,128)(2,1)S(1)}, bf16[128,2560]{1,0:T(8,128)(2,1)S(1)}, u32[]{:S(2)}, u32[]{:S(2)}) collective-permute-start(bf16[128,2560]{1,0:T(8,128)(2,1)S(1)} %collective-permute-done.1.tokens_ref), channel_id=1, source_target_pairs={{0,1},{1,0},{2,3},{3,2},{4,5},{5,4},{6,7},{7,6},{8,9},{9,8},{10,11... | collective-permute-start | bytes 1966088 | tf_op jit(solution)/shard_map/ppermute | solution.py:315
  24.7 12.8 %collective-permute-start.7 = (bf16[3,528,128]{2,1,0:T(8,128)(2,1)S(1)}, bf16[3,528,128]{2,1,0:T(8,128)(2,1)S(1)}, u32[]{:S(2)}, u32[]{:S(2)}) collective-permute-start(bf16[3,528,128]{2,1,0:T(8,128)(2,1)S(1)} %pad_maximum_fusion.2), channel_id=1, source_target_pairs={{0,4},{4,0},{8,12},{12,8},{16,20},{20,16},{24,28},{28,24},{32,36},... | collective-permute-start | bytes 1216520 | tf_op jit(solution)/shard_map/ppermute | solution.py:340
  26.3 11.2 %collective-permute-start.6 = (bf16[2,528,128]{2,1,0:T(8,128)(2,1)S(1)}, bf16[2,528,128]{2,1,0:T(8,128)(2,1)S(1)}, u32[]{:S(2)}, u32[]{:S(2)}) collective-permute-start(bf16[2,528,128]{2,1,0:T(8,128)(2,1)S(1)} %pad_maximum_fusion.6), channel_id=1, source_target_pairs={{0,16},{4,20},{8,24},{12,28},{16,32},{20,36},{24,40},{28,44},{32,4... | collective-permute-start | bytes 811016 | tf_op jit(solution)/shard_map/ppermute | solution.py:312
  26.4 11.1 %collective-permute-start.8 = (bf16[2,528,128]{2,1,0:T(8,128)(2,1)S(1)}, bf16[2,528,128]{2,1,0:T(8,128)(2,1)S(1)}, u32[]{:S(2)}, u32[]{:S(2)}) collective-permute-start(bf16[2,528,128]{2,1,0:T(8,128)(2,1)S(1)} %pad_maximum_fusion.6), channel_id=1, source_target_pairs={{0,12},{4,8},{8,4},{12,0},{16,28},{20,24},{24,20},{28,16},{32,44},... | collective-permute-start | bytes 811016 | tf_op jit(solution)/shard_map/ppermute | solution.py:343
  37.6 12.7 %collective-permute-start.11 = (bf16[3,528,128]{2,1,0:T(8,128)(2,1)S(1)}, bf16[3,528,128]{2,1,0:T(8,128)(2,1)S(1)}, u32[]{:S(2)}, u32[]{:S(2)}) collective-permute-start(bf16[3,528,128]{2,1,0:T(8,128)(2,1)S(1)} %get-tuple-element.39), channel_id=1, source_target_pairs={{0,12},{4,8},{8,4},{12,0},{16,28},{20,24},{24,20},{28,16},{32,44},... | collective-permute-start | bytes 1216520 | tf_op jit(solution)/shard_map/ppermute | solution.py:343
  39.6 9.9 %collective-permute-start.9 = (bf16[2,528,128]{2,1,0:T(8,128)(2,1)S(1)}, bf16[2,528,128]{2,1,0:T(8,128)(2,1)S(1)}, u32[]{:S(2)}, u32[]{:S(2)}) collective-permute-start(bf16[2,528,128]{2,1,0:T(8,128)(2,1)S(1)} %collective-permute-done.6.rest_1_), channel_id=1, source_target_pairs={{0,16},{4,20},{8,24},{12,28},{16,32},{20,36},{24,40},{28,44},{32,4... | collective-permute-start | bytes 811016 | tf_op jit(solution)/shard_map/ppermute | solution.py:312
  39.6 16.5 %collective-permute-start.10 = (bf16[3,528,128]{2,1,0:T(8,128)(2,1)S(1)}, bf16[3,528,128]{2,1,0:T(8,128)(2,1)S(1)}, u32[]{:S(2)}, u32[]{:S(2)}) collective-permute-start(bf16[3,528,128]{2,1,0:T(8,128)(2,1)S(1)} %get-tuple-element.40), channel_id=1, source_target_pairs={{0,4},{4,0},{8,12},{12,8},{16,20},{20,16},{24,28},{28,24},{32,36},... | collective-permute-start | bytes 1216520 | tf_op jit(solution)/shard_map/ppermute | solution.py:340
  49.5 6.6 %collective-permute-start.14 = (bf16[2,528,128]{2,1,0:T(8,128)(2,1)S(1)}, bf16[2,528,128]{2,1,0:T(8,128)(2,1)S(1)}, u32[]{:S(2)}, u32[]{:S(2)}) collective-permute-start(bf16[2,528,128]{2,1,0:T(8,128)(2,1)S(1)} %collective-permute-done.9.rest_1_.rest_0_), channel_id=1, source_target_pairs={{0,12},{4,8},{8,4},{12,0},{16,28},{20,24},{24,20},{28,16},{32,44},... | collective-permute-start | bytes 811016 | tf_op jit(solution)/shard_map/ppermute | solution.py:343
  50.4 9.3 %collective-permute-start.12 = (bf16[2,528,128]{2,1,0:T(8,128)(2,1)S(1)}, bf16[2,528,128]{2,1,0:T(8,128)(2,1)S(1)}, u32[]{:S(2)}, u32[]{:S(2)}) collective-permute-start(bf16[2,528,128]{2,1,0:T(8,128)(2,1)S(1)} %pad_maximum_fusion.7), channel_id=1, source_target_pairs={{0,16},{4,20},{8,24},{12,28},{16,32},{20,36},{24,40},{28,44},{32,4... | collective-permute-start | bytes 811016 | tf_op jit(solution)/shard_map/ppermute | solution.py:312
  50.5 9.4 %collective-permute-start.13 = (bf16[3,528,128]{2,1,0:T(8,128)(2,1)S(1)}, bf16[3,528,128]{2,1,0:T(8,128)(2,1)S(1)}, u32[]{:S(2)}, u32[]{:S(2)}) collective-permute-start(bf16[3,528,128]{2,1,0:T(8,128)(2,1)S(1)} %pad_maximum_fusion.3), channel_id=1, source_target_pairs={{0,4},{4,0},{8,12},{12,8},{16,20},{20,16},{24,28},{28,24},{32,36},... | collective-permute-start | bytes 1216520 | tf_op jit(solution)/shard_map/ppermute | solution.py:340
  59.8 11.3 %collective-permute-start.17 = (bf16[2,528,128]{2,1,0:T(8,128)(2,1)S(1)}, bf16[2,528,128]{2,1,0:T(8,128)(2,1)S(1)}, u32[]{:S(2)}, u32[]{:S(2)}) collective-permute-start(bf16[2,528,128]{2,1,0:T(8,128)(2,1)S(1)} %pad_maximum_fusion.8), channel_id=1, source_target_pairs={{0,16},{4,20},{8,24},{12,28},{16,32},{20,36},{24,40},{28,44},{32,4... | collective-permute-start | bytes 811016 | tf_op jit(solution)/shard_map/ppermute | solution.py:312
  59.9 11.1 %collective-permute-start.15 = (bf16[2,528,128]{2,1,0:T(8,128)(2,1)S(1)}, bf16[2,528,128]{2,1,0:T(8,128)(2,1)S(1)}, u32[]{:S(2)}, u32[]{:S(2)}) collective-permute-start(bf16[2,528,128]{2,1,0:T(8,128)(2,1)S(1)} %get-tuple-element.42), channel_id=1, source_target_pairs={{0,4},{4,0},{8,12},{12,8},{16,20},{20,16},{24,28},{28,24},{32,36},... | collective-permute-start | bytes 811016 | tf_op jit(solution)/shard_map/ppermute | solution.py:340
  60.0 16.4 %collective-permute-start.18 = (bf16[2,528,128]{2,1,0:T(8,128)(2,1)S(1)}, bf16[2,528,128]{2,1,0:T(8,128)(2,1)S(1)}, u32[]{:S(2)}, u32[]{:S(2)}) collective-permute-start(bf16[2,528,128]{2,1,0:T(8,128)(2,1)S(1)} %get-tuple-element.41), channel_id=1, source_target_pairs={{8,20},{12,16},{24,36},{28,32},{40,52},{44,48},{56,68},{60,64},{72... | collective-permute-start | bytes 811016 | tf_op jit(solution)/shard_map/ppermute | solution.py:346
  61.3 9.7 %collective-permute-start.16 = (bf16[1,528,128]{2,1,0:T(8,128)(2,1)S(1)}, bf16[1,528,128]{2,1,0:T(8,128)(2,1)S(1)}, u32[]{:S(2)}, u32[]{:S(2)}) collective-permute-start(bf16[1,528,128]{2,1,0:T(8,128)(2,1)S(1)} %get-tuple-element.36), channel_id=1, source_target_pairs={{0,12},{4,8},{8,4},{12,0},{16,28},{20,24},{24,20},{28,16},{32,44},... | collective-permute-start | bytes 405512 | tf_op jit(solution)/shard_map/ppermute | solution.py:343
  65.3 11.2 %copy-start.1 = (bf16[640,2560]{1,0:T(8,128)(2,1)S(1)}, bf16[640,2560]{1,0:T(8,128)(2,1)}, u32[]{:S(2)}) copy-start(bf16[640,2560]{1,0:T(8,128)(2,1)} %w_ref.3) | copy-start | bytes 9830404
  80.6 6.8 %collective-permute-start.19 = (bf16[128,2560]{1,0:T(8,128)(2,1)S(1)}, bf16[128,2560]{1,0:T(8,128)(2,1)S(1)}, u32[]{:S(2)}, u32[]{:S(2)}) collective-permute-start(bf16[128,2560]{1,0:T(8,128)(2,1)S(1)} %get-tuple-element.29), channel_id=1, source_target_pairs={{0,1},{1,0},{2,3},{3,2},{4,5},{5,4},{6,7},{7,6},{8,9},{9,8},{10,11... | collective-permute-start | bytes 1966088 | tf_op jit(solution)/shard_map/ppermute | solution.py:315
  87.6 16.0 %collective-permute-start.21 = (bf16[128,2560]{1,0:T(8,128)(2,1)S(1)}, bf16[128,2560]{1,0:T(8,128)(2,1)S(1)}, u32[]{:S(2)}, u32[]{:S(2)}) collective-permute-start(bf16[128,2560]{1,0:T(8,128)(2,1)S(1)} %add_convert_fusion.1), channel_id=1, source_target_pairs={{0,2},{1,3},{2,0},{3,1},{4,6},{5,7},{6,4},{7,5},{8,10},{9,11},{10,... | collective-permute-start | bytes 1966088 | tf_op jit(solution)/shard_map/ppermute | solution.py:315
  94.4 9.3 %collective-permute-start.20 = (bf16[128,2560]{1,0:T(8,128)(2,1)S(1)}, bf16[128,2560]{1,0:T(8,128)(2,1)S(1)}, u32[]{:S(2)}, u32[]{:S(2)}) collective-permute-start(bf16[128,2560]{1,0:T(8,128)(2,1)S(1)} %get-tuple-element.32), channel_id=1, source_target_pairs={{0,1},{1,0},{2,3},{3,2},{4,5},{5,4},{6,7},{7,6},{8,9},{9,8},{10,11... | collective-permute-start | bytes 1966088 | tf_op jit(solution)/shard_map/ppermute | solution.py:315
  (1 other events, 0.7 us)
where the time goes:
time: 106 us; the launch traced here: 105 us
  Pallas kernels  37 us (35%)
  waiting for transfers between devices  35.9 us (34%)
  starting transfers between devices  27.2 us (26%)
  other arithmetic  2.09 us (2%)
  local copies, waits for them, and re-layouts  1.97 us (2%)
    pallas_call x6, Pallas kernels, attend(): pl.pallas_call(functools.partial(attend_kernel, target, specs, places, bo...  16.8 us
    ppermute x6, waiting for transfers between devices, across(): return lax.ppermute(x, 'inner', [(i, i ^ flip) for i in range(4)])  15.1 us
    ppermute x5, starting transfers between devices, odd(): return lax.ppermute(x, 'outer', [(i, i ^ 3) for i in ring])  10.9 us
    pallas_call x2, Pallas kernels, attend_last(): pl.pallas_call(functools.partial(last_kernel, target, specs, places, runs...  10.8 us
    ppermute x6, starting transfers between devices, across(): return lax.ppermute(x, 'inner', [(i, i ^ flip) for i in range(4)])  10 us
    ppermute x5, waiting for transfers between devices, along(): lax.ppermute(x, 'outer', [(i, (i + distance) % outer) for i in range(oute...  9.92 us
    ppermute x5, waiting for transfers between devices, odd(): return lax.ppermute(x, 'outer', [(i, i ^ 3) for i in ring])  5.47 us
    ppermute x1, waiting for transfers between devices, corner(): lax.ppermute(x, 'outer', [(i, (i + 7 - 2 * (i % 4)) % outer) for i in rin...  5.43 us
  transfers between devices with their start and end apart: 22, of which 10 were waited for; matrix products, arithmetic and copies ran while one was open for 1% of the time, Pallas kernels for 30%

commit v1 on v0

--- a/solution.py
+++ b/solution.py
@@ -217,13 +217,13 @@
         lax.fori_loop(0, count, one, 0)
 
 
-def attend_kernel(target, specs, places, own, runs, pos_ref, q_ref, *rest):
+def attend_kernel(target, specs, places, own, paired, runs, pos_ref, q_ref, *rest):
     state, msgs, todo = rest[-3:]
     if own:
         attend_all(target, specs, places, rest[2:-3], pos_ref, runs, q_ref, msgs, state, todo, own=rest[:2])
     else:
         state[...] = rest[0][...]
-        attend_all(target, specs, places, rest[1:-3], pos_ref, runs, q_ref, msgs, state, todo)
+        attend_all(target, specs, places, rest[1:-3], pos_ref, runs, q_ref, msgs, state, todo, paired=paired)
 
 
 def unpack(messages):
@@ -248,11 +248,11 @@
     return cost(count * 2 * HEADS * HALF * HALF * HEAD_DIM + more, 2**21, count * HEADS * HALF * HALF // 2)
 
 
-def attend(target, messages, runs, positions, q, state=None, own=()):
+def attend(target, messages, runs, positions, q, state=None, own=(), paired=False):
     specs, places, arrays = unpack(messages)
     before = list(own) if own else [state]
     return pl.pallas_call(
-        functools.partial(attend_kernel, target, specs, places, bool(own), runs),
+        functools.partial(attend_kernel, target, specs, places, bool(own), paired, runs),
         out_shape=jax.ShapeDtypeStruct((STATE, HEADS * HALF), F32),
         in_specs=[SCALARS] + [WHOLE] * (1 + len(before) + len(arrays)),
         out_specs=WHOLE,
@@ -278,7 +278,7 @@
 def last_kernel(target, specs, places, runs, pos_ref, q_ref, state_in, w_ref, *rest):
     keep_ref, send_ref, msgs, todo, state, mixed = rest[-6:]
     state[...] = state_in[...]
-    attend_all(target, specs, places, rest[:-6], pos_ref, runs, q_ref, msgs, state, todo, paired=target == 0)
+    attend_all(target, specs, places, rest[:-6], pos_ref, runs, q_ref, msgs, state, todo, paired=True)
     for h in range(HEADS):
         cols = slice(h * HALF, (h + 1) * HALF)
         scale = 1.0 / state[TOTAL:TOTAL + 1, cols]
@@ -369,10 +369,10 @@
     near_state = attend(A, came1, runs, positions, after(qa, state), own=(a0, b0))
 
     v2 = after(u2, near_state)
-    u3, e3, o3 = up(pack(v2[1:2], o2[2:3])), even(pack(v2, o2[1:2])), odd(v2)
+    u3, e3, o3 = up(pack(v2[1:2], o2[2:3])), even(pack(v2, o2[1:2])), odd(after(v2, e2, o2))
     came3 = ((A, "up", 3, u2, 0), (B, "up", 2, u2, 1), (A, "even", 2, e2, 0), (B, "even", 1, e2, 1),
              (B, "cross", 0, e2, 2), (A, "odd", 2, o2, 0), (B, "odd", 1, o2, 1), (A, "cross", 1, o2, 2))
-    state = attend(B, came3, runs, positions, qb, state)
+    state = attend(B, came3, runs, positions, qb, state, paired=True)
 
     v3 = after(u3, state)
     u4, e4, o4 = up(pack(v3[1:2], o3[0:1])), even(pack(v3[0:1], o3[1:2])), odd(v3[0:1])

time: 106 us -> 104 us (0.981)
    ppermute x5, waiting for transfers between devices: 5.47 us -> 0.01 us  [odd(): return lax.ppermute(x, 'outer', [(i, i ^ 3) for i in ring])]
    ppermute x5, waiting for transfers between devices: 9.92 us -> 14.2 us  [along(): lax.ppermute(x, 'outer', [(i, (i + distance) % outer) for i in range(oute...]
    ppermute x1, waiting for transfers between devices: 5.43 us -> 7.98 us  [corner(): lax.ppermute(x, 'outer', [(i, (i + 7 - 2 * (i % 4)) % outer) for i in rin...]
    ppermute x5, starting transfers between devices: 10.9 us -> 8.37 us  [odd(): return lax.ppermute(x, 'outer', [(i, i ^ 3) for i in ring])]
    ppermute x6, waiting for transfers between devices: 15.1 us -> 13 us  [across(): return lax.ppermute(x, 'inner', [(i, i ^ flip) for i in range(4)])]
    ppermute x6, starting transfers between devices: 10 us -> 11.4 us  [across(): return lax.ppermute(x, 'inner', [(i, i ^ flip) for i in range(4)])]
  transfers between devices with their start and end apart: 22 -> 22, of which waited for: 10 -> 11; matrix products, arithmetic and copies ran while one was open for 1% -> 1% of each run, Pallas kernels for 30% -> 30%
where the time goes in v1:
time: 104 us; the launch traced here: 103 us
  Pallas kernels  36 us (35%)
  waiting for transfers between devices  35.2 us (34%)
  starting transfers between devices  27.1 us (26%)
  other arithmetic  2.2 us (2%)
  local copies, waits for them, and re-layouts  1.97 us (2%)
    pallas_call x6, Pallas kernels, attend(): pl.pallas_call(functools.partial(attend_kernel, target, specs, places, bo...  16.1 us
    ppermute x5, waiting for transfers between devices, along(): lax.ppermute(x, 'outer', [(i, (i + distance) % outer) for i in range(oute...  14.2 us
    ppermute x6, waiting for transfers between devices, across(): return lax.ppermute(x, 'inner', [(i, i ^ flip) for i in range(4)])  13 us
    ppermute x6, starting transfers between devices, across(): return lax.ppermute(x, 'inner', [(i, i ^ flip) for i in range(4)])  11.4 us
    pallas_call x2, Pallas kernels, attend_last(): pl.pallas_call(functools.partial(last_kernel, target, specs, places, runs...  10.5 us
    ppermute x5, starting transfers between devices, odd(): return lax.ppermute(x, 'outer', [(i, i ^ 3) for i in ring])  8.37 us
    ppermute x1, waiting for transfers between devices, corner(): lax.ppermute(x, 'outer', [(i, (i + 7 - 2 * (i % 4)) % outer) for i in rin...  7.98 us
    pallas_call x2, Pallas kernels, project_queries(): pl.pallas_call(functools.partial(query_kernel, half, runs), out_shape=jax...  5.33 us
  transfers between devices with their start and end apart: 22, of which 11 were waited for; matrix products, arithmetic and copies ran while one was open for 1% of the time, Pallas kernels for 30%

profile of v1, /device:TPU:1, one launch (start us, length us, event | category | flops | bytes accessed | tf_op | source)
XLA Modules:
  0.0 102.9 jit_solution(15024972266655457422)
XLA Ops:
  0.0 2.0 %collective-permute-start.1 = (bf16[128,2560]{1,0:T(8,128)(2,1)}, bf16[128,2560]{1,0:T(8,128)(2,1)S(1)}, u32[]{:S(2)}, u32[]{:S(2)}) collective-permute-start(bf16[128,2560]{1,0:T(8,128)(2,1)} %tokens_ref.1), channel_id=1, source_target_pairs={{0,2},{1,3},{2,0},{3,1},{4,6},{5,7},{6,4},{7,5},{8,10},{9,11},{10,... | collective-permute-start | bytes 1966088 | tf_op jit(solution)/shard_map/ppermute | solution.py:315
  4.2 1.4 %collective-permute-start = (bf16[128,2560]{1,0:T(8,128)(2,1)S(1)}, bf16[128,2560]{1,0:T(8,128)(2,1)S(1)}, u32[]{:S(2)}, u32[]{:S(2)}) collective-permute-start(bf16[128,2560]{1,0:T(8,128)(2,1)S(1)} %shard_map.100.own_ref), channel_id=1, source_target_pairs={{0,1},{1,0},{2,3},{3,2},{4,5},{5,4},{6,7},{7,6},{8,9},{9,8},{10,11... | collective-permute-start | bytes 1966088 | tf_op jit(solution)/shard_map/ppermute | solution.py:315
  7.3 1.5 %shard_map.101 = bf16[528,128]{1,0:T(8,128)(2,1)S(1)} custom-call(s32[129]{0:T(256)S(1)} %pad_add_fusion.pos_ref, bf16[128,2560]{1,0:T(8,128)(2,1)S(1)} %shard_map.100.own_ref, bf16[128,2560]{1,0:T(8,128)(2,1)S(1)} %collective-permute-done.other_ref, bf16[2560,128]{1,0:T(8,128)(2,1)S(1)} %copy-done.2, bf16[2560,128]{1,0:T(8,128)(2,1)S(1)} %copy-done.3, ...), custom_call_target="tpu_custom_call" | custom-call | flops 335544320 | bytes 1310720 | tf_op jit(solution)/shard_map/pallas_call | solution.py:109
  8.9 1.4 %collective-permute-start.2 = (bf16[1,528,128]{2,1,0:T(8,128)(2,1)S(1)}, bf16[1,528,128]{2,1,0:T(8,128)(2,1)S(1)}, u32[]{:S(2)}, u32[]{:S(2)}) collective-permute-start(bf16[1,528,128]{2,1,0:T(8,128)(2,1)S(1)} %bitcast.9), channel_id=1, source_target_pairs={{0,16},{4,20},{8,24},{12,28},{16,32},{20,36},{24,40},{28,44},{32,4... | collective-permute-start | bytes 405512 | tf_op jit(solution)/shard_map/ppermute | solution.py:312
  10.3 1.3 %collective-permute-start.3 = (bf16[1,528,128]{2,1,0:T(8,128)(2,1)S(1)}, bf16[1,528,128]{2,1,0:T(8,128)(2,1)S(1)}, u32[]{:S(2)}, u32[]{:S(2)}) collective-permute-start(bf16[1,528,128]{2,1,0:T(8,128)(2,1)S(1)} %bitcast.10), channel_id=1, source_target_pairs={{0,4},{4,0},{8,12},{12,8},{16,20},{20,16},{24,28},{28,24},{32,36},... | collective-permute-start | bytes 405512 | tf_op jit(solution)/shard_map/ppermute | solution.py:340
  11.6 1.9 %collective-permute-start.4 = (bf16[1,528,128]{2,1,0:T(8,128)(2,1)S(1)}, bf16[1,528,128]{2,1,0:T(8,128)(2,1)S(1)}, u32[]{:S(2)}, u32[]{:S(2)}) collective-permute-start(bf16[1,528,128]{2,1,0:T(8,128)(2,1)S(1)} %bitcast.11), channel_id=1, source_target_pairs={{0,12},{4,8},{8,4},{12,0},{16,28},{20,24},{24,20},{28,16},{32,44},... | collective-permute-start | bytes 405512 | tf_op jit(solution)/shard_map/ppermute | solution.py:343
  13.5 2.7 %shard_map.102.q_ref = bf16[128,1280]{1,0:T(8,128)(2,1)S(1)} custom-call(s32[129]{0:T(256)S(1)} %pad_add_fusion.pos_ref, bf16[128,2560]{1,0:T(8,128)(2,1)S(1)} %shard_map.100.own_ref, bf16[128,2560]{1,0:T(8,128)(2,1)S(1)} %collective-permute-done.other_ref, bf16[2560,640]{1,0:T(8,128)(2,1)S(1)} %copy-done, f32[640]{0:T(1024)S(1)} %copy-done.7, ...), custom_call_target="tpu_custom_call" | custom-call | flops 838860800 | bytes 3276800 | tf_op jit(solution)/shard_map/pallas_call | solution.py:122
  16.2 2.2 %collective-permute-done.1.tokens_ref = bf16[128,2560]{1,0:T(8,128)(2,1)S(1)} collective-permute-done((bf16[128,2560]{1,0:T(8,128)(2,1)}, bf16[128,2560]{1,0:T(8,128)(2,1)S(1)}, u32[]{:S(2)}, u32[]{:S(2)}) %collective-permute-start.1) | collective-permute-done | bytes 655392 | tf_op jit(solution)/shard_map/ppermute | solution.py:315
  18.4 1.7 %collective-permute-done.2.rest_2_ = bf16[1,528,128]{2,1,0:T(8,128)(2,1)S(1)} collective-permute-done((bf16[1,528,128]{2,1,0:T(8,128)(2,1)S(1)}, bf16[1,528,128]{2,1,0:T(8,128)(2,1)S(1)}, u32[]{:S(2)}, u32[]{:S(2)}) %collective-permute-start.2) | collective-permute-done | bytes 135200 | tf_op jit(solution)/shard_map/ppermute | solution.py:312
  21.4 1.4 %collective-permute-done.5.tokens_ref = bf16[128,2560]{1,0:T(8,128)(2,1)S(1)} collective-permute-done((bf16[128,2560]{1,0:T(8,128)(2,1)S(1)}, bf16[128,2560]{1,0:T(8,128)(2,1)S(1)}, u32[]{:S(2)}, u32[]{:S(2)}) %collective-permute-start.5) | collective-permute-done | bytes 655392 | tf_op jit(solution)/shard_map/ppermute | solution.py:315
  23.1 1.5 %shard_map.105 = bf16[528,128]{1,0:T(8,128)(2,1)S(1)} custom-call(s32[129]{0:T(256)S(1)} %pad_add_fusion.pos_ref, bf16[128,2560]{1,0:T(8,128)(2,1)S(1)} %shard_map.103.own_ref, bf16[128,2560]{1,0:T(8,128)(2,1)S(1)} %shard_map.104.other_ref, bf16[2560,128]{1,0:T(8,128)(2,1)S(1)} %copy-done.2, bf16[2560,128]{1,0:T(8,128)(2,1)S(1)} %copy-done.3, ...), custom_call_target="tpu_custom_call" | custom-call | flops 335544320 | bytes 1310720 | tf_op jit(solution)/shard_map/pallas_call | solution.py:109
  24.7 1.5 %collective-permute-start.7 = (bf16[3,528,128]{2,1,0:T(8,128)(2,1)S(1)}, bf16[3,528,128]{2,1,0:T(8,128)(2,1)S(1)}, u32[]{:S(2)}, u32[]{:S(2)}) collective-permute-start(bf16[3,528,128]{2,1,0:T(8,128)(2,1)S(1)} %pad_maximum_fusion.2), channel_id=1, source_target_pairs={{0,4},{4,0},{8,12},{12,8},{16,20},{20,16},{24,28},{28,24},{32,36},... | collective-permute-start | bytes 1216520 | tf_op jit(solution)/shard_map/ppermute | solution.py:340
  26.4 2.2 %collective-permute-start.8 = (bf16[2,528,128]{2,1,0:T(8,128)(2,1)S(1)}, bf16[2,528,128]{2,1,0:T(8,128)(2,1)S(1)}, u32[]{:S(2)}, u32[]{:S(2)}) collective-permute-start(bf16[2,528,128]{2,1,0:T(8,128)(2,1)S(1)} %pad_maximum_fusion.6), channel_id=1, source_target_pairs={{0,12},{4,8},{8,4},{12,0},{16,28},{20,24},{24,20},{28,16},{32,44},... | collective-permute-start | bytes 811016 | tf_op jit(solution)/shard_map/ppermute | solution.py:343
  28.5 2.7 %shard_map.106.q_ref = bf16[128,1280]{1,0:T(8,128)(2,1)S(1)} custom-call(s32[129]{0:T(256)S(1)} %pad_add_fusion.pos_ref, bf16[128,2560]{1,0:T(8,128)(2,1)S(1)} %shard_map.103.own_ref, bf16[128,2560]{1,0:T(8,128)(2,1)S(1)} %shard_map.104.other_ref, bf16[2560,640]{1,0:T(8,128)(2,1)S(1)} %copy-done, f32[640]{0:T(1024)S(1)} %copy-done.7, ...), custom_call_target="tpu_custom_call" | custom-call | flops 838860800 | bytes 3276800 | tf_op jit(solution)/shard_map/pallas_call | solution.py:122
  31.2 2.7 %shard_map.107.rest_0_ = f32[144,1280]{1,0:T(8,128)S(1)} custom-call(s32[129]{0:T(256)S(1)} %pad_add_fusion.pos_ref, bf16[128,1280]{1,0:T(8,128)(2,1)S(1)} %shard_map.106.q_ref, bf16[1,528,128]{2,1,0:T(8,128)(2,1)S(1)} %bitcast.12, bf16[1,528,128]{2,1,0:T(8,128)(2,1)S(1)} %bitcast.7, bf16[1,528,128]{2,1,0:T(8,128)(2,1)S(1)} %collective-permute-done.2.rest_2_, ...), custom_call_target="tpu_custom_call" | custom-call | flops 251658240 | bytes 2097152 | tf_op jit(solution)/shard_map/pallas_call | solution.py:254
  33.9 3.6 %collective-permute-done.6.rest_1_ = bf16[2,528,128]{2,1,0:T(8,128)(2,1)S(1)} collective-permute-done((bf16[2,528,128]{2,1,0:T(8,128)(2,1)S(1)}, bf16[2,528,128]{2,1,0:T(8,128)(2,1)S(1)}, u32[]{:S(2)}, u32[]{:S(2)}) %collective-permute-start.6) | collective-permute-done | bytes 270368 | tf_op jit(solution)/shard_map/ppermute | solution.py:312
  37.6 2.0 %collective-permute-start.11 = (bf16[3,528,128]{2,1,0:T(8,128)(2,1)S(1)}, bf16[3,528,128]{2,1,0:T(8,128)(2,1)S(1)}, u32[]{:S(2)}, u32[]{:S(2)}) collective-permute-start(bf16[3,528,128]{2,1,0:T(8,128)(2,1)S(1)} %get-tuple-element.41), channel_id=1, source_target_pairs={{0,12},{4,8},{8,4},{12,0},{16,28},{20,24},{24,20},{28,16},{32,44},... | collective-permute-start | bytes 1216520 | tf_op jit(solution)/shard_map/ppermute | solution.py:343
  40.0 2.8 %shard_map.108.rest_0_ = f32[144,1280]{1,0:T(8,128)S(1)} custom-call(s32[129]{0:T(256)S(1)} %pad_add_fusion.pos_ref, bf16[128,1280]{1,0:T(8,128)(2,1)S(1)} %shard_map.106.q_ref, f32[144,1280]{1,0:T(8,128)S(1)} %shard_map.107.rest_0_, bf16[2,528,128]{2,1,0:T(8,128)(2,1)S(1)} %collective-permute-done.6.rest_1_, ...), custom_call_target="tpu_custom_call" | custom-call | flops 587202560 | bytes 2097152 | tf_op jit(solution)/shard_map/pallas_call | solution.py:254
  42.8 1.9 %shard_map.110.rest_0_ = f32[144,1280]{1,0:T(8,128)S(1)} custom-call(s32[129]{0:T(256)S(1)} %pad_add_fusion.pos_ref, bf16[128,1280]{1,0:T(8,128)(2,1)S(1)} %shard_map.102.q_ref, bf16[1,528,128]{2,1,0:T(8,128)(2,1)S(1)} %bitcast.13, bf16[1,528,128]{2,1,0:T(8,128)(2,1)S(1)} %bitcast.8, bf16[1,528,128]{2,1,0:T(8,128)(2,1)S(1)} %collective-permute-done.2.rest_2_, ...), custom_call_target="tpu_custom_call" | custom-call | flops 251658240 | bytes 2097152 | tf_op jit(solution)/shard_map/pallas_call | solution.py:254
  44.8 4.7 %collective-permute-done.9.rest_1_.rest_0_ = bf16[2,528,128]{2,1,0:T(8,128)(2,1)S(1)} collective-permute-done((bf16[2,528,128]{2,1,0:T(8,128)(2,1)S(1)}, bf16[2,528,128]{2,1,0:T(8,128)(2,1)S(1)}, u32[]{:S(2)}, u32[]{:S(2)}) %collective-permute-start.9) | collective-permute-done | bytes 270368 | tf_op jit(solution)/shard_map/ppermute | solution.py:312
  51.1 3.7 %shard_map.109.rest_0_ = f32[144,1280]{1,0:T(8,128)S(1)} custom-call(s32[129]{0:T(256)S(1)} %pad_add_fusion.pos_ref, bf16[128,1280]{1,0:T(8,128)(2,1)S(1)} %shard_map.106.q_ref, f32[144,1280]{1,0:T(8,128)S(1)} %shard_map.108.rest_0_, bf16[2,528,128]{2,1,0:T(8,128)(2,1)S(1)} %collective-permute-done.9.rest_1_.rest_0_, ...), custom_call_target="tpu_custom_call" | custom-call | flops 671088640 | bytes 2097152 | tf_op jit(solution)/shard_map/pallas_call | solution.py:254
  54.8 3.7 %collective-permute-done.12.rest_1_.rest_3_ = bf16[2,528,128]{2,1,0:T(8,128)(2,1)S(1)} collective-permute-done((bf16[2,528,128]{2,1,0:T(8,128)(2,1)S(1)}, bf16[2,528,128]{2,1,0:T(8,128)(2,1)S(1)}, u32[]{:S(2)}, u32[]{:S(2)}) %collective-permute-start.12) | collective-permute-done | bytes 270368 | tf_op jit(solution)/shard_map/ppermute | solution.py:312
  60.8 1.3 %collective-permute-start.16 = (bf16[1,528,128]{2,1,0:T(8,128)(2,1)S(1)}, bf16[1,528,128]{2,1,0:T(8,128)(2,1)S(1)}, u32[]{:S(2)}, u32[]{:S(2)}) collective-permute-start(bf16[1,528,128]{2,1,0:T(8,128)(2,1)S(1)} %get-tuple-element.38), channel_id=1, source_target_pairs={{0,12},{4,8},{8,4},{12,0},{16,28},{20,24},{24,20},{28,16},{32,44},... | collective-permute-start | bytes 405512 | tf_op jit(solution)/shard_map/ppermute | solution.py:343
  62.1 2.8 %shard_map.111.state_in = f32[144,1280]{1,0:T(8,128)S(1)} custom-call(s32[129]{0:T(256)S(1)} %pad_add_fusion.pos_ref, bf16[128,1280]{1,0:T(8,128)(2,1)S(1)} %shard_map.106.q_ref, f32[144,1280]{1,0:T(8,128)S(1)} %shard_map.109.rest_0_, bf16[2,528,128]{2,1,0:T(8,128)(2,1)S(1)} %collective-permute-done.12.rest_1_.rest_3_, ...), custom_call_target="tpu_custom_call" | custom-call | flops 587202560 | bytes 2097152 | tf_op jit(solution)/shard_map/pallas_call | solution.py:254
  65.0 2.1 %shard_map.112.state_in = f32[144,1280]{1,0:T(8,128)S(1)} custom-call(s32[129]{0:T(256)S(1)} %pad_add_fusion.pos_ref, bf16[128,1280]{1,0:T(8,128)(2,1)S(1)} %shard_map.102.q_ref, f32[144,1280]{1,0:T(8,128)S(1)} %shard_map.110.rest_0_, bf16[2,528,128]{2,1,0:T(8,128)(2,1)S(1)} %collective-permute-done.6.rest_1_, ...), custom_call_target="tpu_custom_call" | custom-call | flops 587202560 | bytes 2097152 | tf_op jit(solution)/shard_map/pallas_call | solution.py:254
  67.6 8.0 %collective-permute-done.18.rest_3_.rest_9_ = bf16[2,528,128]{2,1,0:T(8,128)(2,1)S(1)} collective-permute-done((bf16[2,528,128]{2,1,0:T(8,128)(2,1)S(1)}, bf16[2,528,128]{2,1,0:T(8,128)(2,1)S(1)}, u32[]{:S(2)}, u32[]{:S(2)}) %collective-permute-start.18) | collective-permute-done | bytes 270368 | tf_op jit(solution)/shard_map/ppermute | solution.py:346
  75.6 3.1 %shard_map.113 = (bf16[128,2560]{1,0:T(8,128)(2,1)S(1)}, bf16[128,2560]{1,0:T(8,128)(2,1)S(1)}) custom-call(s32[129]{0:T(256)S(1)} %pad_add_fusion.pos_ref, bf16[128,1280]{1,0:T(8,128)(2,1)S(1)} %shard_map.106.q_ref, f32[144,1280]{1,0:T(8,128)S(1)} %shard_map.111.state_in, bf16[640,2560]{1,0:T(8,128)(2,1)S(1)} %copy-done.1, ...), custom_call_target="tpu_custom_call" | custom-call | flops 1426063360 | bytes 2097152 | tf_op jit(solution)/shard_map/pallas_call | solution.py:292
  78.8 3.3 %collective-permute-start.19 = (bf16[128,2560]{1,0:T(8,128)(2,1)S(1)}, bf16[128,2560]{1,0:T(8,128)(2,1)S(1)}, u32[]{:S(2)}, u32[]{:S(2)}) collective-permute-start(bf16[128,2560]{1,0:T(8,128)(2,1)S(1)} %get-tuple-element.31), channel_id=1, source_target_pairs={{0,1},{1,0},{2,3},{3,2},{4,5},{5,4},{6,7},{7,6},{8,9},{9,8},{10,11... | collective-permute-start | bytes 1966088 | tf_op jit(solution)/shard_map/ppermute | solution.py:315
  82.1 1.7 %collective-permute-done.19 = bf16[128,2560]{1,0:T(8,128)(2,1)S(1)} collective-permute-done((bf16[128,2560]{1,0:T(8,128)(2,1)S(1)}, bf16[128,2560]{1,0:T(8,128)(2,1)S(1)}, u32[]{:S(2)}, u32[]{:S(2)}) %collective-permute-start.19) | collective-permute-done | bytes 655392 | tf_op jit(solution)/shard_map/ppermute | solution.py:315
  84.0 3.0 %collective-permute-start.21 = (bf16[128,2560]{1,0:T(8,128)(2,1)S(1)}, bf16[128,2560]{1,0:T(8,128)(2,1)S(1)}, u32[]{:S(2)}, u32[]{:S(2)}) collective-permute-start(bf16[128,2560]{1,0:T(8,128)(2,1)S(1)} %add_convert_fusion.1), channel_id=1, source_target_pairs={{0,2},{1,3},{2,0},{3,1},{4,6},{5,7},{6,4},{7,5},{8,10},{9,11},{10,... | collective-permute-start | bytes 1966088 | tf_op jit(solution)/shard_map/ppermute | solution.py:315
  87.0 7.3 %shard_map.114 = (bf16[128,2560]{1,0:T(8,128)(2,1)S(1)}, bf16[128,2560]{1,0:T(8,128)(2,1)S(1)}) custom-call(s32[129]{0:T(256)S(1)} %pad_add_fusion.pos_ref, bf16[128,1280]{1,0:T(8,128)(2,1)S(1)} %shard_map.102.q_ref, f32[144,1280]{1,0:T(8,128)S(1)} %shard_map.112.state_in, bf16[640,2560]{1,0:T(8,128)(2,1)S(1)} %copy-done.1, ...), custom_call_target="tpu_custom_call" | custom-call | flops 2684354560 | bytes 2097152 | tf_op jit(solution)/shard_map/pallas_call | solution.py:292
  95.1 6.7 %collective-permute-done.21 = bf16[128,2560]{1,0:T(8,128)(2,1)S(1)} collective-permute-done((bf16[128,2560]{1,0:T(8,128)(2,1)S(1)}, bf16[128,2560]{1,0:T(8,128)(2,1)S(1)}, u32[]{:S(2)}, u32[]{:S(2)}) %collective-permute-start.21) | collective-permute-done | bytes 655392 | tf_op jit(solution)/shard_map/ppermute | solution.py:315
  (70 shorter events, 12.4 us)
Async XLA Ops:
  0.0 7.3 %copy-start.2 = (bf16[2560,128]{1,0:T(8,128)(2,1)S(1)}, bf16[2560,128]{1,0:T(8,128)(2,1)}, u32[]{:S(2)}) copy-start(bf16[2560,128]{1,0:T(8,128)(2,1)} %wk_ref.3) | copy-start | bytes 1966084
  0.0 7.3 %copy-start.3 = (bf16[2560,128]{1,0:T(8,128)(2,1)S(1)}, bf16[2560,128]{1,0:T(8,128)(2,1)}, u32[]{:S(2)}) copy-start(bf16[2560,128]{1,0:T(8,128)(2,1)} %wv_ref.3) | copy-start | bytes 1966084
  0.0 18.4 %collective-permute-start.1 = (bf16[128,2560]{1,0:T(8,128)(2,1)}, bf16[128,2560]{1,0:T(8,128)(2,1)S(1)}, u32[]{:S(2)}, u32[]{:S(2)}) collective-permute-start(bf16[128,2560]{1,0:T(8,128)(2,1)} %tokens_ref.1), channel_id=1, source_target_pairs={{0,2},{1,3},{2,0},{3,1},{4,6},{5,7},{6,4},{7,5},{8,10},{9,11},{10,... | collective-permute-start | bytes 1966088 | tf_op jit(solution)/shard_map/ppermute | solution.py:315
  2.0 1.1 %copy-start.4 = (bf16[128,2560]{1,0:T(8,128)(2,1)S(1)}, bf16[128,2560]{1,0:T(8,128)(2,1)}, u32[]{:S(2)}) copy-start(bf16[128,2560]{1,0:T(8,128)(2,1)} %tokens_ref.1) | copy-start | bytes 1966084
  3.9 1.8 %copy-start.10 = (s32[128]{0:T(128)S(1)}, s32[128]{0:T(128)}, u32[]{:S(2)}) copy-start(s32[128]{0:T(128)} %param.19) | copy-start | bytes 1540
  3.9 3.4 %copy-start.8 = (f32[128]{0:T(128)S(1)}, f32[128]{0:T(128)}, u32[]{:S(2)}) copy-start(f32[128]{0:T(128)} %bk_ref.3) | copy-start | bytes 1540
  3.9 3.4 %copy-start.9 = (f32[128]{0:T(128)S(1)}, f32[128]{0:T(128)}, u32[]{:S(2)}) copy-start(f32[128]{0:T(128)} %bv_ref.3) | copy-start | bytes 1540
  4.2 3.1 %collective-permute-start = (bf16[128,2560]{1,0:T(8,128)(2,1)S(1)}, bf16[128,2560]{1,0:T(8,128)(2,1)S(1)}, u32[]{:S(2)}, u32[]{:S(2)}) collective-permute-start(bf16[128,2560]{1,0:T(8,128)(2,1)S(1)} %shard_map.100.own_ref), channel_id=1, source_target_pairs={{0,1},{1,0},{2,3},{3,2},{4,5},{5,4},{6,7},{7,6},{8,9},{9,8},{10,11... | collective-permute-start | bytes 1966088 | tf_op jit(solution)/shard_map/ppermute | solution.py:315
  5.9 7.6 %copy-start = (bf16[2560,640]{1,0:T(8,128)(2,1)S(1)}, bf16[2560,640]{1,0:T(8,128)(2,1)}, u32[]{:S(2)}) copy-start(bf16[2560,640]{1,0:T(8,128)(2,1)} %wq_ref.3) | copy-start | bytes 9830404
  7.3 6.2 %copy-start.7 = (f32[640]{0:T(1024)S(1)}, f32[640]{0:T(1024)}, u32[]{:S(2)}) copy-start(f32[640]{0:T(1024)} %bq_ref.3) | copy-start | bytes 7684
  8.9 12.2 %copy-start.6 = (f32[2560]{0:T(1024)S(1)}, f32[2560]{0:T(1024)}, u32[]{:S(2)}) copy-start(f32[2560]{0:T(1024)} %gain_ref.5) | copy-start | bytes 30724
  8.9 11.2 %collective-permute-start.2 = (bf16[1,528,128]{2,1,0:T(8,128)(2,1)S(1)}, bf16[1,528,128]{2,1,0:T(8,128)(2,1)S(1)}, u32[]{:S(2)}, u32[]{:S(2)}) collective-permute-start(bf16[1,528,128]{2,1,0:T(8,128)(2,1)S(1)} %bitcast.9), channel_id=1, source_target_pairs={{0,16},{4,20},{8,24},{12,28},{16,32},{20,36},{24,40},{28,44},{32,4... | collective-permute-start | bytes 405512 | tf_op jit(solution)/shard_map/ppermute | solution.py:312
  10.3 9.8 %collective-permute-start.3 = (bf16[1,528,128]{2,1,0:T(8,128)(2,1)S(1)}, bf16[1,528,128]{2,1,0:T(8,128)(2,1)S(1)}, u32[]{:S(2)}, u32[]{:S(2)}) collective-permute-start(bf16[1,528,128]{2,1,0:T(8,128)(2,1)S(1)} %bitcast.10), channel_id=1, source_target_pairs={{0,4},{4,0},{8,12},{12,8},{16,20},{20,16},{24,28},{28,24},{32,36},... | collective-permute-start | bytes 405512 | tf_op jit(solution)/shard_map/ppermute | solution.py:340
  11.6 8.5 %collective-permute-start.4 = (bf16[1,528,128]{2,1,0:T(8,128)(2,1)S(1)}, bf16[1,528,128]{2,1,0:T(8,128)(2,1)S(1)}, u32[]{:S(2)}, u32[]{:S(2)}) collective-permute-start(bf16[1,528,128]{2,1,0:T(8,128)(2,1)S(1)} %bitcast.11), channel_id=1, source_target_pairs={{0,12},{4,8},{8,4},{12,0},{16,28},{20,24},{24,20},{28,16},{32,44},... | collective-permute-start | bytes 405512 | tf_op jit(solution)/shard_map/ppermute | solution.py:343
  20.1 2.7 %collective-permute-start.5 = (bf16[128,2560]{1,0:T(8,128)(2,1)S(1)}, bf16[128,2560]{1,0:T(8,128)(2,1)S(1)}, u32[]{:S(2)}, u32[]{:S(2)}) collective-permute-start(bf16[128,2560]{1,0:T(8,128)(2,1)S(1)} %collective-permute-done.1.tokens_ref), channel_id=1, source_target_pairs={{0,1},{1,0},{2,3},{3,2},{4,5},{5,4},{6,7},{7,6},{8,9},{9,8},{10,11... | collective-permute-start | bytes 1966088 | tf_op jit(solution)/shard_map/ppermute | solution.py:315
  24.7 12.8 %collective-permute-start.7 = (bf16[3,528,128]{2,1,0:T(8,128)(2,1)S(1)}, bf16[3,528,128]{2,1,0:T(8,128)(2,1)S(1)}, u32[]{:S(2)}, u32[]{:S(2)}) collective-permute-start(bf16[3,528,128]{2,1,0:T(8,128)(2,1)S(1)} %pad_maximum_fusion.2), channel_id=1, source_target_pairs={{0,4},{4,0},{8,12},{12,8},{16,20},{20,16},{24,28},{28,24},{32,36},... | collective-permute-start | bytes 1216520 | tf_op jit(solution)/shard_map/ppermute | solution.py:340
  26.3 11.2 %collective-permute-start.6 = (bf16[2,528,128]{2,1,0:T(8,128)(2,1)S(1)}, bf16[2,528,128]{2,1,0:T(8,128)(2,1)S(1)}, u32[]{:S(2)}, u32[]{:S(2)}) collective-permute-start(bf16[2,528,128]{2,1,0:T(8,128)(2,1)S(1)} %pad_maximum_fusion.6), channel_id=1, source_target_pairs={{0,16},{4,20},{8,24},{12,28},{16,32},{20,36},{24,40},{28,44},{32,4... | collective-permute-start | bytes 811016 | tf_op jit(solution)/shard_map/ppermute | solution.py:312
  26.4 11.1 %collective-permute-start.8 = (bf16[2,528,128]{2,1,0:T(8,128)(2,1)S(1)}, bf16[2,528,128]{2,1,0:T(8,128)(2,1)S(1)}, u32[]{:S(2)}, u32[]{:S(2)}) collective-permute-start(bf16[2,528,128]{2,1,0:T(8,128)(2,1)S(1)} %pad_maximum_fusion.6), channel_id=1, source_target_pairs={{0,12},{4,8},{8,4},{12,0},{16,28},{20,24},{24,20},{28,16},{32,44},... | collective-permute-start | bytes 811016 | tf_op jit(solution)/shard_map/ppermute | solution.py:343
  37.6 11.9 %collective-permute-start.11 = (bf16[3,528,128]{2,1,0:T(8,128)(2,1)S(1)}, bf16[3,528,128]{2,1,0:T(8,128)(2,1)S(1)}, u32[]{:S(2)}, u32[]{:S(2)}) collective-permute-start(bf16[3,528,128]{2,1,0:T(8,128)(2,1)S(1)} %get-tuple-element.41), channel_id=1, source_target_pairs={{0,12},{4,8},{8,4},{12,0},{16,28},{20,24},{24,20},{28,16},{32,44},... | collective-permute-start | bytes 1216520 | tf_op jit(solution)/shard_map/ppermute | solution.py:343
  39.6 9.9 %collective-permute-start.9 = (bf16[2,528,128]{2,1,0:T(8,128)(2,1)S(1)}, bf16[2,528,128]{2,1,0:T(8,128)(2,1)S(1)}, u32[]{:S(2)}, u32[]{:S(2)}) collective-permute-start(bf16[2,528,128]{2,1,0:T(8,128)(2,1)S(1)} %collective-permute-done.6.rest_1_), channel_id=1, source_target_pairs={{0,16},{4,20},{8,24},{12,28},{16,32},{20,36},{24,40},{28,44},{32,4... | collective-permute-start | bytes 811016 | tf_op jit(solution)/shard_map/ppermute | solution.py:312
  39.6 10.6 %collective-permute-start.10 = (bf16[3,528,128]{2,1,0:T(8,128)(2,1)S(1)}, bf16[3,528,128]{2,1,0:T(8,128)(2,1)S(1)}, u32[]{:S(2)}, u32[]{:S(2)}) collective-permute-start(bf16[3,528,128]{2,1,0:T(8,128)(2,1)S(1)} %get-tuple-element.42), channel_id=1, source_target_pairs={{0,4},{4,0},{8,12},{12,8},{16,20},{20,16},{24,28},{28,24},{32,36},... | collective-permute-start | bytes 1216520 | tf_op jit(solution)/shard_map/ppermute | solution.py:340
  49.5 9.0 %collective-permute-start.12 = (bf16[2,528,128]{2,1,0:T(8,128)(2,1)S(1)}, bf16[2,528,128]{2,1,0:T(8,128)(2,1)S(1)}, u32[]{:S(2)}, u32[]{:S(2)}) collective-permute-start(bf16[2,528,128]{2,1,0:T(8,128)(2,1)S(1)} %pad_maximum_fusion.7), channel_id=1, source_target_pairs={{0,16},{4,20},{8,24},{12,28},{16,32},{20,36},{24,40},{28,44},{32,4... | collective-permute-start | bytes 811016 | tf_op jit(solution)/shard_map/ppermute | solution.py:312
  49.7 9.1 %collective-permute-start.13 = (bf16[3,528,128]{2,1,0:T(8,128)(2,1)S(1)}, bf16[3,528,128]{2,1,0:T(8,128)(2,1)S(1)}, u32[]{:S(2)}, u32[]{:S(2)}) collective-permute-start(bf16[3,528,128]{2,1,0:T(8,128)(2,1)S(1)} %pad_maximum_fusion.3), channel_id=1, source_target_pairs={{0,4},{4,0},{8,12},{12,8},{16,20},{20,16},{24,28},{28,24},{32,36},... | collective-permute-start | bytes 1216520 | tf_op jit(solution)/shard_map/ppermute | solution.py:340
  50.2 8.4 %collective-permute-start.14 = (bf16[2,528,128]{2,1,0:T(8,128)(2,1)S(1)}, bf16[2,528,128]{2,1,0:T(8,128)(2,1)S(1)}, u32[]{:S(2)}, u32[]{:S(2)}) collective-permute-start(bf16[2,528,128]{2,1,0:T(8,128)(2,1)S(1)} %collective-permute-done.9.rest_1_.rest_0_), channel_id=1, source_target_pairs={{0,12},{4,8},{8,4},{12,0},{16,28},{20,24},{24,20},{28,16},{32,44},... | collective-permute-start | bytes 811016 | tf_op jit(solution)/shard_map/ppermute | solution.py:343
  58.6 9.0 %collective-permute-start.17 = (bf16[2,528,128]{2,1,0:T(8,128)(2,1)S(1)}, bf16[2,528,128]{2,1,0:T(8,128)(2,1)S(1)}, u32[]{:S(2)}, u32[]{:S(2)}) collective-permute-start(bf16[2,528,128]{2,1,0:T(8,128)(2,1)S(1)} %pad_maximum_fusion.8), channel_id=1, source_target_pairs={{0,16},{4,20},{8,24},{12,28},{16,32},{20,36},{24,40},{28,44},{32,4... | collective-permute-start | bytes 811016 | tf_op jit(solution)/shard_map/ppermute | solution.py:312
  58.8 8.8 %collective-permute-start.15 = (bf16[2,528,128]{2,1,0:T(8,128)(2,1)S(1)}, bf16[2,528,128]{2,1,0:T(8,128)(2,1)S(1)}, u32[]{:S(2)}, u32[]{:S(2)}) collective-permute-start(bf16[2,528,128]{2,1,0:T(8,128)(2,1)S(1)} %get-tuple-element.44), channel_id=1, source_target_pairs={{0,4},{4,0},{8,12},{12,8},{16,20},{20,16},{24,28},{28,24},{32,36},... | collective-permute-start | bytes 811016 | tf_op jit(solution)/shard_map/ppermute | solution.py:340
  59.5 16.1 %collective-permute-start.18 = (bf16[2,528,128]{2,1,0:T(8,128)(2,1)S(1)}, bf16[2,528,128]{2,1,0:T(8,128)(2,1)S(1)}, u32[]{:S(2)}, u32[]{:S(2)}) collective-permute-start(bf16[2,528,128]{2,1,0:T(8,128)(2,1)S(1)} %get-tuple-element.43), channel_id=1, source_target_pairs={{8,20},{12,16},{24,36},{28,32},{40,52},{44,48},{56,68},{60,64},{72... | collective-permute-start | bytes 811016 | tf_op jit(solution)/shard_map/ppermute | solution.py:346
  60.8 6.3 %collective-permute-start.16 = (bf16[1,528,128]{2,1,0:T(8,128)(2,1)S(1)}, bf16[1,528,128]{2,1,0:T(8,128)(2,1)S(1)}, u32[]{:S(2)}, u32[]{:S(2)}) collective-permute-start(bf16[1,528,128]{2,1,0:T(8,128)(2,1)S(1)} %get-tuple-element.38), channel_id=1, source_target_pairs={{0,12},{4,8},{8,4},{12,0},{16,28},{20,24},{24,20},{28,16},{32,44},... | collective-permute-start | bytes 405512 | tf_op jit(solution)/shard_map/ppermute | solution.py:343
  62.1 13.5 %copy-start.1 = (bf16[640,2560]{1,0:T(8,128)(2,1)S(1)}, bf16[640,2560]{1,0:T(8,128)(2,1)}, u32[]{:S(2)}) copy-start(bf16[640,2560]{1,0:T(8,128)(2,1)} %w_ref.3) | copy-start | bytes 9830404
  78.8 5.0 %collective-permute-start.19 = (bf16[128,2560]{1,0:T(8,128)(2,1)S(1)}, bf16[128,2560]{1,0:T(8,128)(2,1)S(1)}, u32[]{:S(2)}, u32[]{:S(2)}) collective-permute-start(bf16[128,2560]{1,0:T(8,128)(2,1)S(1)} %get-tuple-element.31), channel_id=1, source_target_pairs={{0,1},{1,0},{2,3},{3,2},{4,5},{5,4},{6,7},{7,6},{8,9},{9,8},{10,11... | collective-permute-start | bytes 1966088 | tf_op jit(solution)/shard_map/ppermute | solution.py:315
  84.0 17.8 %collective-permute-start.21 = (bf16[128,2560]{1,0:T(8,128)(2,1)S(1)}, bf16[128,2560]{1,0:T(8,128)(2,1)S(1)}, u32[]{:S(2)}, u32[]{:S(2)}) collective-permute-start(bf16[128,2560]{1,0:T(8,128)(2,1)S(1)} %add_convert_fusion.1), channel_id=1, source_target_pairs={{0,2},{1,3},{2,0},{3,1},{4,6},{5,7},{6,4},{7,5},{8,10},{9,11},{10,... | collective-permute-start | bytes 1966088 | tf_op jit(solution)/shard_map/ppermute | solution.py:315
  94.3 7.5 %collective-permute-start.20 = (bf16[128,2560]{1,0:T(8,128)(2,1)S(1)}, bf16[128,2560]{1,0:T(8,128)(2,1)S(1)}, u32[]{:S(2)}, u32[]{:S(2)}) collective-permute-start(bf16[128,2560]{1,0:T(8,128)(2,1)S(1)} %get-tuple-element.34), channel_id=1, source_target_pairs={{0,1},{1,0},{2,3},{3,2},{4,5},{5,4},{6,7},{7,6},{8,9},{9,8},{10,11... | collective-permute-start | bytes 1966088 | tf_op jit(solution)/shard_map/ppermute | solution.py:315
  (1 other events, 0.7 us)

commit v2 on v1

--- a/solution.py
+++ b/solution.py
@@ -380,7 +380,7 @@
     came4 = ((B, "up", 3, u3, 0), (A, "cross", 2, u3, 1), (A, "even", 3, e3, 0), (B, "even", 2, e3, 1),
              (B, "cross", 1, e3, 2), (A, "odd", 3, o3, 0), (B, "odd", 2, o3, 1))
     state = attend(B, came4, runs, positions, qb, state)
-    near_state = attend(A, came2, runs, positions, after(qa, state), near_state)
+    near_state = attend(A, came2 + came3[:4], runs, positions, after(qa, state), near_state)
     came5 = ((B, "even", 3, e4, 0), (B, "cross", 2, e4, 1), (B, "odd", 3, o4, 0), (A, "cross", 3, u4, 0),
              (A, "corner", 3, u4, 1), (B, "corner", 3, c4, 0), (B, "cross", 3, c4, 1))
 
@@ -389,7 +389,7 @@
     other = (keep_far.astype(F32) + got_far.astype(F32)).astype(BF16)
     arrived = across(other, 2)
     keep_near, send_near = attend_last(
-        A, came3 + came4 + came5, runs, positions, after(qa, other), near_state, w_out
+        A, came3[4:] + came4 + came5, runs, positions, after(qa, other), near_state, w_out
     )
     got_near = across(send_near, 1)
     return (keep_near.astype(F32) + got_near.astype(F32) + arrived.astype(F32)).astype(BF16)

time: 104 us -> 103 us (level); the launches traced: 103 us -> 103 us
  waiting for transfers between devices: 35.2 us -> 38.2 us
  starting transfers between devices: 27.1 us -> 24.5 us
    ppermute x6, waiting for transfers between devices: 13 us -> 18.5 us  [across(): return lax.ppermute(x, 'inner', [(i, i ^ flip) for i in range(4)])]
    ppermute x6, starting transfers between devices: 11.4 us -> 8.22 us  [across(): return lax.ppermute(x, 'inner', [(i, i ^ flip) for i in range(4)])]
    pallas_call x6, Pallas kernels: 16.1 us -> 18 us  [attend(): pl.pallas_call(functools.partial(attend_kernel, target, specs, places, bo...]
    pallas_call x2, Pallas kernels: 10.5 us -> 8.59 us  [attend_last(): pl.pallas_call(functools.partial(last_kernel, target, specs, places, runs...]
    ppermute x1, waiting for transfers between devices: 7.98 us -> 6.42 us  [corner(): lax.ppermute(x, 'outer', [(i, (i + 7 - 2 * (i % 4)) % outer) for i in rin...]
  transfers between devices with their start and end apart: 22 -> 22, of which waited for: 11 -> 10; matrix products, arithmetic and copies ran while one was open for 1% -> 1% of each run, Pallas kernels for 30% -> 28%
where the time goes in v2:
time: 103 us
  waiting for transfers between devices  38.2 us (37%)
  Pallas kernels  36 us (35%)
  starting transfers between devices  24.5 us (24%)
  other arithmetic  2.08 us (2%)
  local copies, waits for them, and re-layouts  1.97 us (2%)
    ppermute x6, waiting for transfers between devices, across(): return lax.ppermute(x, 'inner', [(i, i ^ flip) for i in range(4)])  18.5 us
    pallas_call x6, Pallas kernels, attend(): pl.pallas_call(functools.partial(attend_kernel, target, specs, places, bo...  18 us
    ppermute x5, waiting for transfers between devices, along(): lax.ppermute(x, 'outer', [(i, (i + distance) % outer) for i in range(oute...  13.2 us
    ppermute x5, starting transfers between devices, odd(): return lax.ppermute(x, 'outer', [(i, i ^ 3) for i in ring])  8.97 us
    pallas_call x2, Pallas kernels, attend_last(): pl.pallas_call(functools.partial(last_kernel, target, specs, places, runs...  8.59 us
    ppermute x6, starting transfers between devices, across(): return lax.ppermute(x, 'inner', [(i, i ^ flip) for i in range(4)])  8.22 us
    ppermute x1, waiting for transfers between devices, corner(): lax.ppermute(x, 'outer', [(i, (i + 7 - 2 * (i % 4)) % outer) for i in rin...  6.42 us
    pallas_call x2, Pallas kernels, project_queries(): pl.pallas_call(functools.partial(query_kernel, half, runs), out_shape=jax...  5.33 us
  transfers between devices with their start and end apart: 22, of which 10 were waited for; matrix products, arithmetic and copies ran while one was open for 1% of the time, Pallas kernels for 28%

profile of v2, /device:TPU:1, one launch (start us, length us, event | category | flops | bytes accessed | tf_op | source)
XLA Modules:
  0.0 103.3 jit_solution(7554423459419715437)
XLA Ops:
  0.0 2.0 %collective-permute-start.1 = (bf16[128,2560]{1,0:T(8,128)(2,1)}, bf16[128,2560]{1,0:T(8,128)(2,1)S(1)}, u32[]{:S(2)}, u32[]{:S(2)}) collective-permute-start(bf16[128,2560]{1,0:T(8,128)(2,1)} %tokens_ref.1), channel_id=1, source_target_pairs={{0,2},{1,3},{2,0},{3,1},{4,6},{5,7},{6,4},{7,5},{8,10},{9,11},{10,... | collective-permute-start | bytes 1966088 | tf_op jit(solution)/shard_map/ppermute | solution.py:315
  4.2 1.4 %collective-permute-start = (bf16[128,2560]{1,0:T(8,128)(2,1)S(1)}, bf16[128,2560]{1,0:T(8,128)(2,1)S(1)}, u32[]{:S(2)}, u32[]{:S(2)}) collective-permute-start(bf16[128,2560]{1,0:T(8,128)(2,1)S(1)} %shard_map.100.own_ref), channel_id=1, source_target_pairs={{0,1},{1,0},{2,3},{3,2},{4,5},{5,4},{6,7},{7,6},{8,9},{9,8},{10,11... | collective-permute-start | bytes 1966088 | tf_op jit(solution)/shard_map/ppermute | solution.py:315
  7.3 1.5 %shard_map.101 = bf16[528,128]{1,0:T(8,128)(2,1)S(1)} custom-call(s32[129]{0:T(256)S(1)} %pad_add_fusion.pos_ref, bf16[128,2560]{1,0:T(8,128)(2,1)S(1)} %shard_map.100.own_ref, bf16[128,2560]{1,0:T(8,128)(2,1)S(1)} %collective-permute-done.other_ref, bf16[2560,128]{1,0:T(8,128)(2,1)S(1)} %copy-done.2, bf16[2560,128]{1,0:T(8,128)(2,1)S(1)} %copy-done.3, ...), custom_call_target="tpu_custom_call" | custom-call | flops 335544320 | bytes 1310720 | tf_op jit(solution)/shard_map/pallas_call | solution.py:109
  8.9 1.4 %collective-permute-start.2 = (bf16[1,528,128]{2,1,0:T(8,128)(2,1)S(1)}, bf16[1,528,128]{2,1,0:T(8,128)(2,1)S(1)}, u32[]{:S(2)}, u32[]{:S(2)}) collective-permute-start(bf16[1,528,128]{2,1,0:T(8,128)(2,1)S(1)} %bitcast.9), channel_id=1, source_target_pairs={{0,16},{4,20},{8,24},{12,28},{16,32},{20,36},{24,40},{28,44},{32,4... | collective-permute-start | bytes 405512 | tf_op jit(solution)/shard_map/ppermute | solution.py:312
  10.3 1.3 %collective-permute-start.3 = (bf16[1,528,128]{2,1,0:T(8,128)(2,1)S(1)}, bf16[1,528,128]{2,1,0:T(8,128)(2,1)S(1)}, u32[]{:S(2)}, u32[]{:S(2)}) collective-permute-start(bf16[1,528,128]{2,1,0:T(8,128)(2,1)S(1)} %bitcast.10), channel_id=1, source_target_pairs={{0,4},{4,0},{8,12},{12,8},{16,20},{20,16},{24,28},{28,24},{32,36},... | collective-permute-start | bytes 405512 | tf_op jit(solution)/shard_map/ppermute | solution.py:340
  11.6 1.9 %collective-permute-start.4 = (bf16[1,528,128]{2,1,0:T(8,128)(2,1)S(1)}, bf16[1,528,128]{2,1,0:T(8,128)(2,1)S(1)}, u32[]{:S(2)}, u32[]{:S(2)}) collective-permute-start(bf16[1,528,128]{2,1,0:T(8,128)(2,1)S(1)} %bitcast.11), channel_id=1, source_target_pairs={{0,12},{4,8},{8,4},{12,0},{16,28},{20,24},{24,20},{28,16},{32,44},... | collective-permute-start | bytes 405512 | tf_op jit(solution)/shard_map/ppermute | solution.py:343
  13.5 2.7 %shard_map.102.q_ref = bf16[128,1280]{1,0:T(8,128)(2,1)S(1)} custom-call(s32[129]{0:T(256)S(1)} %pad_add_fusion.pos_ref, bf16[128,2560]{1,0:T(8,128)(2,1)S(1)} %shard_map.100.own_ref, bf16[128,2560]{1,0:T(8,128)(2,1)S(1)} %collective-permute-done.other_ref, bf16[2560,640]{1,0:T(8,128)(2,1)S(1)} %copy-done, f32[640]{0:T(1024)S(1)} %copy-done.7, ...), custom_call_target="tpu_custom_call" | custom-call | flops 838860800 | bytes 3276800 | tf_op jit(solution)/shard_map/pallas_call | solution.py:122
  16.2 2.2 %collective-permute-done.1.tokens_ref = bf16[128,2560]{1,0:T(8,128)(2,1)S(1)} collective-permute-done((bf16[128,2560]{1,0:T(8,128)(2,1)}, bf16[128,2560]{1,0:T(8,128)(2,1)S(1)}, u32[]{:S(2)}, u32[]{:S(2)}) %collective-permute-start.1) | collective-permute-done | bytes 655392 | tf_op jit(solution)/shard_map/ppermute | solution.py:315
  18.4 1.7 %collective-permute-done.2.rest_2_ = bf16[1,528,128]{2,1,0:T(8,128)(2,1)S(1)} collective-permute-done((bf16[1,528,128]{2,1,0:T(8,128)(2,1)S(1)}, bf16[1,528,128]{2,1,0:T(8,128)(2,1)S(1)}, u32[]{:S(2)}, u32[]{:S(2)}) %collective-permute-start.2) | collective-permute-done | bytes 135200 | tf_op jit(solution)/shard_map/ppermute | solution.py:312
  21.4 1.4 %collective-permute-done.5.tokens_ref = bf16[128,2560]{1,0:T(8,128)(2,1)S(1)} collective-permute-done((bf16[128,2560]{1,0:T(8,128)(2,1)S(1)}, bf16[128,2560]{1,0:T(8,128)(2,1)S(1)}, u32[]{:S(2)}, u32[]{:S(2)}) %collective-permute-start.5) | collective-permute-done | bytes 655392 | tf_op jit(solution)/shard_map/ppermute | solution.py:315
  23.1 1.5 %shard_map.105 = bf16[528,128]{1,0:T(8,128)(2,1)S(1)} custom-call(s32[129]{0:T(256)S(1)} %pad_add_fusion.pos_ref, bf16[128,2560]{1,0:T(8,128)(2,1)S(1)} %shard_map.103.own_ref, bf16[128,2560]{1,0:T(8,128)(2,1)S(1)} %shard_map.104.other_ref, bf16[2560,128]{1,0:T(8,128)(2,1)S(1)} %copy-done.2, bf16[2560,128]{1,0:T(8,128)(2,1)S(1)} %copy-done.3, ...), custom_call_target="tpu_custom_call" | custom-call | flops 335544320 | bytes 1310720 | tf_op jit(solution)/shard_map/pallas_call | solution.py:109
  24.7 1.5 %collective-permute-start.7 = (bf16[3,528,128]{2,1,0:T(8,128)(2,1)S(1)}, bf16[3,528,128]{2,1,0:T(8,128)(2,1)S(1)}, u32[]{:S(2)}, u32[]{:S(2)}) collective-permute-start(bf16[3,528,128]{2,1,0:T(8,128)(2,1)S(1)} %pad_maximum_fusion.2), channel_id=1, source_target_pairs={{0,4},{4,0},{8,12},{12,8},{16,20},{20,16},{24,28},{28,24},{32,36},... | collective-permute-start | bytes 1216520 | tf_op jit(solution)/shard_map/ppermute | solution.py:340
  26.4 2.2 %collective-permute-start.8 = (bf16[2,528,128]{2,1,0:T(8,128)(2,1)S(1)}, bf16[2,528,128]{2,1,0:T(8,128)(2,1)S(1)}, u32[]{:S(2)}, u32[]{:S(2)}) collective-permute-start(bf16[2,528,128]{2,1,0:T(8,128)(2,1)S(1)} %pad_maximum_fusion.6), channel_id=1, source_target_pairs={{0,12},{4,8},{8,4},{12,0},{16,28},{20,24},{24,20},{28,16},{32,44},... | collective-permute-start | bytes 811016 | tf_op jit(solution)/shard_map/ppermute | solution.py:343
  28.5 2.7 %shard_map.106.q_ref = bf16[128,1280]{1,0:T(8,128)(2,1)S(1)} custom-call(s32[129]{0:T(256)S(1)} %pad_add_fusion.pos_ref, bf16[128,2560]{1,0:T(8,128)(2,1)S(1)} %shard_map.103.own_ref, bf16[128,2560]{1,0:T(8,128)(2,1)S(1)} %shard_map.104.other_ref, bf16[2560,640]{1,0:T(8,128)(2,1)S(1)} %copy-done, f32[640]{0:T(1024)S(1)} %copy-done.7, ...), custom_call_target="tpu_custom_call" | custom-call | flops 838860800 | bytes 3276800 | tf_op jit(solution)/shard_map/pallas_call | solution.py:122
  31.2 2.7 %shard_map.107.rest_0_ = f32[144,1280]{1,0:T(8,128)S(1)} custom-call(s32[129]{0:T(256)S(1)} %pad_add_fusion.pos_ref, bf16[128,1280]{1,0:T(8,128)(2,1)S(1)} %shard_map.106.q_ref, bf16[1,528,128]{2,1,0:T(8,128)(2,1)S(1)} %bitcast.12, bf16[1,528,128]{2,1,0:T(8,128)(2,1)S(1)} %bitcast.7, bf16[1,528,128]{2,1,0:T(8,128)(2,1)S(1)} %collective-permute-done.2.rest_2_, ...), custom_call_target="tpu_custom_call" | custom-call | flops 251658240 | bytes 2097152 | tf_op jit(solution)/shard_map/pallas_call | solution.py:254
  33.9 3.6 %collective-permute-done.6.rest_1_ = bf16[2,528,128]{2,1,0:T(8,128)(2,1)S(1)} collective-permute-done((bf16[2,528,128]{2,1,0:T(8,128)(2,1)S(1)}, bf16[2,528,128]{2,1,0:T(8,128)(2,1)S(1)}, u32[]{:S(2)}, u32[]{:S(2)}) %collective-permute-start.6) | collective-permute-done | bytes 270368 | tf_op jit(solution)/shard_map/ppermute | solution.py:312
  37.6 2.0 %collective-permute-start.11 = (bf16[3,528,128]{2,1,0:T(8,128)(2,1)S(1)}, bf16[3,528,128]{2,1,0:T(8,128)(2,1)S(1)}, u32[]{:S(2)}, u32[]{:S(2)}) collective-permute-start(bf16[3,528,128]{2,1,0:T(8,128)(2,1)S(1)} %get-tuple-element.41), channel_id=1, source_target_pairs={{0,12},{4,8},{8,4},{12,0},{16,28},{20,24},{24,20},{28,16},{32,44},... | collective-permute-start | bytes 1216520 | tf_op jit(solution)/shard_map/ppermute | solution.py:343
  40.0 2.9 %shard_map.108.rest_0_ = f32[144,1280]{1,0:T(8,128)S(1)} custom-call(s32[129]{0:T(256)S(1)} %pad_add_fusion.pos_ref, bf16[128,1280]{1,0:T(8,128)(2,1)S(1)} %shard_map.106.q_ref, f32[144,1280]{1,0:T(8,128)S(1)} %shard_map.107.rest_0_, bf16[2,528,128]{2,1,0:T(8,128)(2,1)S(1)} %collective-permute-done.6.rest_1_, ...), custom_call_target="tpu_custom_call" | custom-call | flops 587202560 | bytes 2097152 | tf_op jit(solution)/shard_map/pallas_call | solution.py:254
  42.8 1.9 %shard_map.110.rest_0_ = f32[144,1280]{1,0:T(8,128)S(1)} custom-call(s32[129]{0:T(256)S(1)} %pad_add_fusion.pos_ref, bf16[128,1280]{1,0:T(8,128)(2,1)S(1)} %shard_map.102.q_ref, bf16[1,528,128]{2,1,0:T(8,128)(2,1)S(1)} %bitcast.13, bf16[1,528,128]{2,1,0:T(8,128)(2,1)S(1)} %bitcast.8, bf16[1,528,128]{2,1,0:T(8,128)(2,1)S(1)} %collective-permute-done.2.rest_2_, ...), custom_call_target="tpu_custom_call" | custom-call | flops 251658240 | bytes 2097152 | tf_op jit(solution)/shard_map/pallas_call | solution.py:254
  44.8 4.6 %collective-permute-done.9.rest_1_.rest_4_ = bf16[2,528,128]{2,1,0:T(8,128)(2,1)S(1)} collective-permute-done((bf16[2,528,128]{2,1,0:T(8,128)(2,1)S(1)}, bf16[2,528,128]{2,1,0:T(8,128)(2,1)S(1)}, u32[]{:S(2)}, u32[]{:S(2)}) %collective-permute-start.9) | collective-permute-done | bytes 270368 | tf_op jit(solution)/shard_map/ppermute | solution.py:312
  51.1 4.1 %shard_map.109.rest_0_ = f32[144,1280]{1,0:T(8,128)S(1)} custom-call(s32[129]{0:T(256)S(1)} %pad_add_fusion.pos_ref, bf16[128,1280]{1,0:T(8,128)(2,1)S(1)} %shard_map.106.q_ref, f32[144,1280]{1,0:T(8,128)S(1)} %shard_map.108.rest_0_, bf16[2,528,128]{2,1,0:T(8,128)(2,1)S(1)} %collective-permute-done.9.rest_1_.rest_4_, ...), custom_call_target="tpu_custom_call" | custom-call | flops 671088640 | bytes 2097152 | tf_op jit(solution)/shard_map/pallas_call | solution.py:254
  55.3 3.3 %collective-permute-done.12.rest_1_.rest_2_ = bf16[2,528,128]{2,1,0:T(8,128)(2,1)S(1)} collective-permute-done((bf16[2,528,128]{2,1,0:T(8,128)(2,1)S(1)}, bf16[2,528,128]{2,1,0:T(8,128)(2,1)S(1)}, u32[]{:S(2)}, u32[]{:S(2)}) %collective-permute-start.12) | collective-permute-done | bytes 270368 | tf_op jit(solution)/shard_map/ppermute | solution.py:312
  59.5 1.3 %collective-permute-start.18 = (bf16[2,528,128]{2,1,0:T(8,128)(2,1)S(1)}, bf16[2,528,128]{2,1,0:T(8,128)(2,1)S(1)}, u32[]{:S(2)}, u32[]{:S(2)}) collective-permute-start(bf16[2,528,128]{2,1,0:T(8,128)(2,1)S(1)} %get-tuple-element.43), channel_id=1, source_target_pairs={{8,20},{12,16},{24,36},{28,32},{40,52},{44,48},{56,68},{60,64},{72... | collective-permute-start | bytes 811016 | tf_op jit(solution)/shard_map/ppermute | solution.py:346
  60.8 1.9 %collective-permute-start.16 = (bf16[1,528,128]{2,1,0:T(8,128)(2,1)S(1)}, bf16[1,528,128]{2,1,0:T(8,128)(2,1)S(1)}, u32[]{:S(2)}, u32[]{:S(2)}) collective-permute-start(bf16[1,528,128]{2,1,0:T(8,128)(2,1)S(1)} %get-tuple-element.38), channel_id=1, source_target_pairs={{0,12},{4,8},{8,4},{12,0},{16,28},{20,24},{24,20},{28,16},{32,44},... | collective-permute-start | bytes 405512 | tf_op jit(solution)/shard_map/ppermute | solution.py:343
  62.7 4.2 %shard_map.111.state_in = f32[144,1280]{1,0:T(8,128)S(1)} custom-call(s32[129]{0:T(256)S(1)} %pad_add_fusion.pos_ref, bf16[128,1280]{1,0:T(8,128)(2,1)S(1)} %shard_map.106.q_ref, f32[144,1280]{1,0:T(8,128)S(1)} %shard_map.109.rest_0_, bf16[2,528,128]{2,1,0:T(8,128)(2,1)S(1)} %collective-permute-done.12.rest_1_.rest_2_, ...), custom_call_target="tpu_custom_call" | custom-call | flops 587202560 | bytes 2097152 | tf_op jit(solution)/shard_map/pallas_call | solution.py:254
  67.0 2.2 %shard_map.112.state_in = f32[144,1280]{1,0:T(8,128)S(1)} custom-call(s32[129]{0:T(256)S(1)} %pad_add_fusion.pos_ref, bf16[128,1280]{1,0:T(8,128)(2,1)S(1)} %shard_map.102.q_ref, f32[144,1280]{1,0:T(8,128)S(1)} %shard_map.110.rest_0_, bf16[2,528,128]{2,1,0:T(8,128)(2,1)S(1)} %collective-permute-done.6.rest_1_, ...), custom_call_target="tpu_custom_call" | custom-call | flops 922746880 | bytes 2097152 | tf_op jit(solution)/shard_map/pallas_call | solution.py:254
  69.2 6.4 %collective-permute-done.18.rest_3_.rest_8_ = bf16[2,528,128]{2,1,0:T(8,128)(2,1)S(1)} collective-permute-done((bf16[2,528,128]{2,1,0:T(8,128)(2,1)S(1)}, bf16[2,528,128]{2,1,0:T(8,128)(2,1)S(1)}, u32[]{:S(2)}, u32[]{:S(2)}) %collective-permute-start.18) | collective-permute-done | bytes 270368 | tf_op jit(solution)/shard_map/ppermute | solution.py:346
  75.6 5.4 %shard_map.113 = (bf16[128,2560]{1,0:T(8,128)(2,1)S(1)}, bf16[128,2560]{1,0:T(8,128)(2,1)S(1)}) custom-call(s32[129]{0:T(256)S(1)} %pad_add_fusion.pos_ref, bf16[128,1280]{1,0:T(8,128)(2,1)S(1)} %shard_map.106.q_ref, f32[144,1280]{1,0:T(8,128)S(1)} %shard_map.111.state_in, bf16[640,2560]{1,0:T(8,128)(2,1)S(1)} %copy-done.1, ...), custom_call_target="tpu_custom_call" | custom-call | flops 1426063360 | bytes 2097152 | tf_op jit(solution)/shard_map/pallas_call | solution.py:292
  81.0 3.3 %collective-permute-start.19 = (bf16[128,2560]{1,0:T(8,128)(2,1)S(1)}, bf16[128,2560]{1,0:T(8,128)(2,1)S(1)}, u32[]{:S(2)}, u32[]{:S(2)}) collective-permute-start(bf16[128,2560]{1,0:T(8,128)(2,1)S(1)} %get-tuple-element.31), channel_id=1, source_target_pairs={{0,1},{1,0},{2,3},{3,2},{4,5},{5,4},{6,7},{7,6},{8,9},{9,8},{10,11... | collective-permute-start | bytes 1966088 | tf_op jit(solution)/shard_map/ppermute | solution.py:315
  84.3 1.7 %collective-permute-done.19 = bf16[128,2560]{1,0:T(8,128)(2,1)S(1)} collective-permute-done((bf16[128,2560]{1,0:T(8,128)(2,1)S(1)}, bf16[128,2560]{1,0:T(8,128)(2,1)S(1)}, u32[]{:S(2)}, u32[]{:S(2)}) %collective-permute-start.19) | collective-permute-done | bytes 655392 | tf_op jit(solution)/shard_map/ppermute | solution.py:315
  86.3 3.2 %shard_map.114 = (bf16[128,2560]{1,0:T(8,128)(2,1)S(1)}, bf16[128,2560]{1,0:T(8,128)(2,1)S(1)}) custom-call(s32[129]{0:T(256)S(1)} %pad_add_fusion.pos_ref, bf16[128,1280]{1,0:T(8,128)(2,1)S(1)} %shard_map.102.q_ref, f32[144,1280]{1,0:T(8,128)S(1)} %shard_map.112.state_in, bf16[640,2560]{1,0:T(8,128)(2,1)S(1)} %copy-done.1, ...), custom_call_target="tpu_custom_call" | custom-call | flops 2348810240 | bytes 2097152 | tf_op jit(solution)/shard_map/pallas_call | solution.py:292
  90.0 12.3 %collective-permute-done.21 = bf16[128,2560]{1,0:T(8,128)(2,1)S(1)} collective-permute-done((bf16[128,2560]{1,0:T(8,128)(2,1)S(1)}, bf16[128,2560]{1,0:T(8,128)(2,1)S(1)}, u32[]{:S(2)}, u32[]{:S(2)}) %collective-permute-start.21) | collective-permute-done | bytes 655392 | tf_op jit(solution)/shard_map/ppermute | solution.py:315
  (70 shorter events, 10.4 us)
Async XLA Ops:
  0.0 7.3 %copy-start.2 = (bf16[2560,128]{1,0:T(8,128)(2,1)S(1)}, bf16[2560,128]{1,0:T(8,128)(2,1)}, u32[]{:S(2)}) copy-start(bf16[2560,128]{1,0:T(8,128)(2,1)} %wk_ref.3) | copy-start | bytes 1966084
  0.0 7.3 %copy-start.3 = (bf16[2560,128]{1,0:T(8,128)(2,1)S(1)}, bf16[2560,128]{1,0:T(8,128)(2,1)}, u32[]{:S(2)}) copy-start(bf16[2560,128]{1,0:T(8,128)(2,1)} %wv_ref.3) | copy-start | bytes 1966084
  0.0 18.4 %collective-permute-start.1 = (bf16[128,2560]{1,0:T(8,128)(2,1)}, bf16[128,2560]{1,0:T(8,128)(2,1)S(1)}, u32[]{:S(2)}, u32[]{:S(2)}) collective-permute-start(bf16[128,2560]{1,0:T(8,128)(2,1)} %tokens_ref.1), channel_id=1, source_target_pairs={{0,2},{1,3},{2,0},{3,1},{4,6},{5,7},{6,4},{7,5},{8,10},{9,11},{10,... | collective-permute-start | bytes 1966088 | tf_op jit(solution)/shard_map/ppermute | solution.py:315
  2.0 1.1 %copy-start.4 = (bf16[128,2560]{1,0:T(8,128)(2,1)S(1)}, bf16[128,2560]{1,0:T(8,128)(2,1)}, u32[]{:S(2)}) copy-start(bf16[128,2560]{1,0:T(8,128)(2,1)} %tokens_ref.1) | copy-start | bytes 1966084
  3.9 1.8 %copy-start.10 = (s32[128]{0:T(128)S(1)}, s32[128]{0:T(128)}, u32[]{:S(2)}) copy-start(s32[128]{0:T(128)} %param.19) | copy-start | bytes 1540
  3.9 3.4 %copy-start.8 = (f32[128]{0:T(128)S(1)}, f32[128]{0:T(128)}, u32[]{:S(2)}) copy-start(f32[128]{0:T(128)} %bk_ref.3) | copy-start | bytes 1540
  3.9 3.4 %copy-start.9 = (f32[128]{0:T(128)S(1)}, f32[128]{0:T(128)}, u32[]{:S(2)}) copy-start(f32[128]{0:T(128)} %bv_ref.3) | copy-start | bytes 1540
  4.2 3.1 %collective-permute-start = (bf16[128,2560]{1,0:T(8,128)(2,1)S(1)}, bf16[128,2560]{1,0:T(8,128)(2,1)S(1)}, u32[]{:S(2)}, u32[]{:S(2)}) collective-permute-start(bf16[128,2560]{1,0:T(8,128)(2,1)S(1)} %shard_map.100.own_ref), channel_id=1, source_target_pairs={{0,1},{1,0},{2,3},{3,2},{4,5},{5,4},{6,7},{7,6},{8,9},{9,8},{10,11... | collective-permute-start | bytes 1966088 | tf_op jit(solution)/shard_map/ppermute | solution.py:315
  5.9 7.6 %copy-start = (bf16[2560,640]{1,0:T(8,128)(2,1)S(1)}, bf16[2560,640]{1,0:T(8,128)(2,1)}, u32[]{:S(2)}) copy-start(bf16[2560,640]{1,0:T(8,128)(2,1)} %wq_ref.3) | copy-start | bytes 9830404
  7.3 6.2 %copy-start.7 = (f32[640]{0:T(1024)S(1)}, f32[640]{0:T(1024)}, u32[]{:S(2)}) copy-start(f32[640]{0:T(1024)} %bq_ref.3) | copy-start | bytes 7684
  8.9 12.2 %copy-start.6 = (f32[2560]{0:T(1024)S(1)}, f32[2560]{0:T(1024)}, u32[]{:S(2)}) copy-start(f32[2560]{0:T(1024)} %gain_ref.5) | copy-start | bytes 30724
  8.9 11.2 %collective-permute-start.2 = (bf16[1,528,128]{2,1,0:T(8,128)(2,1)S(1)}, bf16[1,528,128]{2,1,0:T(8,128)(2,1)S(1)}, u32[]{:S(2)}, u32[]{:S(2)}) collective-permute-start(bf16[1,528,128]{2,1,0:T(8,128)(2,1)S(1)} %bitcast.9), channel_id=1, source_target_pairs={{0,16},{4,20},{8,24},{12,28},{16,32},{20,36},{24,40},{28,44},{32,4... | collective-permute-start | bytes 405512 | tf_op jit(solution)/shard_map/ppermute | solution.py:312
  10.3 9.8 %collective-permute-start.3 = (bf16[1,528,128]{2,1,0:T(8,128)(2,1)S(1)}, bf16[1,528,128]{2,1,0:T(8,128)(2,1)S(1)}, u32[]{:S(2)}, u32[]{:S(2)}) collective-permute-start(bf16[1,528,128]{2,1,0:T(8,128)(2,1)S(1)} %bitcast.10), channel_id=1, source_target_pairs={{0,4},{4,0},{8,12},{12,8},{16,20},{20,16},{24,28},{28,24},{32,36},... | collective-permute-start | bytes 405512 | tf_op jit(solution)/shard_map/ppermute | solution.py:340
  11.6 8.5 %collective-permute-start.4 = (bf16[1,528,128]{2,1,0:T(8,128)(2,1)S(1)}, bf16[1,528,128]{2,1,0:T(8,128)(2,1)S(1)}, u32[]{:S(2)}, u32[]{:S(2)}) collective-permute-start(bf16[1,528,128]{2,1,0:T(8,128)(2,1)S(1)} %bitcast.11), channel_id=1, source_target_pairs={{0,12},{4,8},{8,4},{12,0},{16,28},{20,24},{24,20},{28,16},{32,44},... | collective-permute-start | bytes 405512 | tf_op jit(solution)/shard_map/ppermute | solution.py:343
  20.1 2.7 %collective-permute-start.5 = (bf16[128,2560]{1,0:T(8,128)(2,1)S(1)}, bf16[128,2560]{1,0:T(8,128)(2,1)S(1)}, u32[]{:S(2)}, u32[]{:S(2)}) collective-permute-start(bf16[128,2560]{1,0:T(8,128)(2,1)S(1)} %collective-permute-done.1.tokens_ref), channel_id=1, source_target_pairs={{0,1},{1,0},{2,3},{3,2},{4,5},{5,4},{6,7},{7,6},{8,9},{9,8},{10,11... | collective-permute-start | bytes 1966088 | tf_op jit(solution)/shard_map/ppermute | solution.py:315
  24.7 12.8 %collective-permute-start.7 = (bf16[3,528,128]{2,1,0:T(8,128)(2,1)S(1)}, bf16[3,528,128]{2,1,0:T(8,128)(2,1)S(1)}, u32[]{:S(2)}, u32[]{:S(2)}) collective-permute-start(bf16[3,528,128]{2,1,0:T(8,128)(2,1)S(1)} %pad_maximum_fusion.2), channel_id=1, source_target_pairs={{0,4},{4,0},{8,12},{12,8},{16,20},{20,16},{24,28},{28,24},{32,36},... | collective-permute-start | bytes 1216520 | tf_op jit(solution)/shard_map/ppermute | solution.py:340
  26.3 11.2 %collective-permute-start.6 = (bf16[2,528,128]{2,1,0:T(8,128)(2,1)S(1)}, bf16[2,528,128]{2,1,0:T(8,128)(2,1)S(1)}, u32[]{:S(2)}, u32[]{:S(2)}) collective-permute-start(bf16[2,528,128]{2,1,0:T(8,128)(2,1)S(1)} %pad_maximum_fusion.6), channel_id=1, source_target_pairs={{0,16},{4,20},{8,24},{12,28},{16,32},{20,36},{24,40},{28,44},{32,4... | collective-permute-start | bytes 811016 | tf_op jit(solution)/shard_map/ppermute | solution.py:312
  26.4 11.1 %collective-permute-start.8 = (bf16[2,528,128]{2,1,0:T(8,128)(2,1)S(1)}, bf16[2,528,128]{2,1,0:T(8,128)(2,1)S(1)}, u32[]{:S(2)}, u32[]{:S(2)}) collective-permute-start(bf16[2,528,128]{2,1,0:T(8,128)(2,1)S(1)} %pad_maximum_fusion.6), channel_id=1, source_target_pairs={{0,12},{4,8},{8,4},{12,0},{16,28},{20,24},{24,20},{28,16},{32,44},... | collective-permute-start | bytes 811016 | tf_op jit(solution)/shard_map/ppermute | solution.py:343
  37.6 11.9 %collective-permute-start.11 = (bf16[3,528,128]{2,1,0:T(8,128)(2,1)S(1)}, bf16[3,528,128]{2,1,0:T(8,128)(2,1)S(1)}, u32[]{:S(2)}, u32[]{:S(2)}) collective-permute-start(bf16[3,528,128]{2,1,0:T(8,128)(2,1)S(1)} %get-tuple-element.41), channel_id=1, source_target_pairs={{0,12},{4,8},{8,4},{12,0},{16,28},{20,24},{24,20},{28,16},{32,44},... | collective-permute-start | bytes 1216520 | tf_op jit(solution)/shard_map/ppermute | solution.py:343
  39.6 9.9 %collective-permute-start.9 = (bf16[2,528,128]{2,1,0:T(8,128)(2,1)S(1)}, bf16[2,528,128]{2,1,0:T(8,128)(2,1)S(1)}, u32[]{:S(2)}, u32[]{:S(2)}) collective-permute-start(bf16[2,528,128]{2,1,0:T(8,128)(2,1)S(1)} %collective-permute-done.6.rest_1_), channel_id=1, source_target_pairs={{0,16},{4,20},{8,24},{12,28},{16,32},{20,36},{24,40},{28,44},{32,4... | collective-permute-start | bytes 811016 | tf_op jit(solution)/shard_map/ppermute | solution.py:312
  39.6 10.6 %collective-permute-start.10 = (bf16[3,528,128]{2,1,0:T(8,128)(2,1)S(1)}, bf16[3,528,128]{2,1,0:T(8,128)(2,1)S(1)}, u32[]{:S(2)}, u32[]{:S(2)}) collective-permute-start(bf16[3,528,128]{2,1,0:T(8,128)(2,1)S(1)} %get-tuple-element.42), channel_id=1, source_target_pairs={{0,4},{4,0},{8,12},{12,8},{16,20},{20,16},{24,28},{28,24},{32,36},... | collective-permute-start | bytes 1216520 | tf_op jit(solution)/shard_map/ppermute | solution.py:340
  49.5 9.0 %collective-permute-start.12 = (bf16[2,528,128]{2,1,0:T(8,128)(2,1)S(1)}, bf16[2,528,128]{2,1,0:T(8,128)(2,1)S(1)}, u32[]{:S(2)}, u32[]{:S(2)}) collective-permute-start(bf16[2,528,128]{2,1,0:T(8,128)(2,1)S(1)} %pad_maximum_fusion.7), channel_id=1, source_target_pairs={{0,16},{4,20},{8,24},{12,28},{16,32},{20,36},{24,40},{28,44},{32,4... | collective-permute-start | bytes 811016 | tf_op jit(solution)/shard_map/ppermute | solution.py:312
  49.7 9.1 %collective-permute-start.13 = (bf16[3,528,128]{2,1,0:T(8,128)(2,1)S(1)}, bf16[3,528,128]{2,1,0:T(8,128)(2,1)S(1)}, u32[]{:S(2)}, u32[]{:S(2)}) collective-permute-start(bf16[3,528,128]{2,1,0:T(8,128)(2,1)S(1)} %pad_maximum_fusion.3), channel_id=1, source_target_pairs={{0,4},{4,0},{8,12},{12,8},{16,20},{20,16},{24,28},{28,24},{32,36},... | collective-permute-start | bytes 1216520 | tf_op jit(solution)/shard_map/ppermute | solution.py:340
  50.2 8.4 %collective-permute-start.14 = (bf16[2,528,128]{2,1,0:T(8,128)(2,1)S(1)}, bf16[2,528,128]{2,1,0:T(8,128)(2,1)S(1)}, u32[]{:S(2)}, u32[]{:S(2)}) collective-permute-start(bf16[2,528,128]{2,1,0:T(8,128)(2,1)S(1)} %collective-permute-done.9.rest_1_.rest_4_), channel_id=1, source_target_pairs={{0,12},{4,8},{8,4},{12,0},{16,28},{20,24},{24,20},{28,16},{32,44},... | collective-permute-start | bytes 811016 | tf_op jit(solution)/shard_map/ppermute | solution.py:343
  58.6 10.5 %collective-permute-start.17 = (bf16[2,528,128]{2,1,0:T(8,128)(2,1)S(1)}, bf16[2,528,128]{2,1,0:T(8,128)(2,1)S(1)}, u32[]{:S(2)}, u32[]{:S(2)}) collective-permute-start(bf16[2,528,128]{2,1,0:T(8,128)(2,1)S(1)} %pad_maximum_fusion.8), channel_id=1, source_target_pairs={{0,16},{4,20},{8,24},{12,28},{16,32},{20,36},{24,40},{28,44},{32,4... | collective-permute-start | bytes 811016 | tf_op jit(solution)/shard_map/ppermute | solution.py:312
  58.8 10.4 %collective-permute-start.15 = (bf16[2,528,128]{2,1,0:T(8,128)(2,1)S(1)}, bf16[2,528,128]{2,1,0:T(8,128)(2,1)S(1)}, u32[]{:S(2)}, u32[]{:S(2)}) collective-permute-start(bf16[2,528,128]{2,1,0:T(8,128)(2,1)S(1)} %get-tuple-element.44), channel_id=1, source_target_pairs={{0,4},{4,0},{8,12},{12,8},{16,20},{20,16},{24,28},{28,24},{32,36},... | collective-permute-start | bytes 811016 | tf_op jit(solution)/shard_map/ppermute | solution.py:340
  59.5 16.1 %collective-permute-start.18 = (bf16[2,528,128]{2,1,0:T(8,128)(2,1)S(1)}, bf16[2,528,128]{2,1,0:T(8,128)(2,1)S(1)}, u32[]{:S(2)}, u32[]{:S(2)}) collective-permute-start(bf16[2,528,128]{2,1,0:T(8,128)(2,1)S(1)} %get-tuple-element.43), channel_id=1, source_target_pairs={{8,20},{12,16},{24,36},{28,32},{40,52},{44,48},{56,68},{60,64},{72... | collective-permute-start | bytes 811016 | tf_op jit(solution)/shard_map/ppermute | solution.py:346
  60.8 8.4 %collective-permute-start.16 = (bf16[1,528,128]{2,1,0:T(8,128)(2,1)S(1)}, bf16[1,528,128]{2,1,0:T(8,128)(2,1)S(1)}, u32[]{:S(2)}, u32[]{:S(2)}) collective-permute-start(bf16[1,528,128]{2,1,0:T(8,128)(2,1)S(1)} %get-tuple-element.38), channel_id=1, source_target_pairs={{0,12},{4,8},{8,4},{12,0},{16,28},{20,24},{24,20},{28,16},{32,44},... | collective-permute-start | bytes 405512 | tf_op jit(solution)/shard_map/ppermute | solution.py:343
  67.0 8.6 %copy-start.1 = (bf16[640,2560]{1,0:T(8,128)(2,1)S(1)}, bf16[640,2560]{1,0:T(8,128)(2,1)}, u32[]{:S(2)}) copy-start(bf16[640,2560]{1,0:T(8,128)(2,1)} %w_ref.3) | copy-start | bytes 9830404
  81.0 5.0 %collective-permute-start.19 = (bf16[128,2560]{1,0:T(8,128)(2,1)S(1)}, bf16[128,2560]{1,0:T(8,128)(2,1)S(1)}, u32[]{:S(2)}, u32[]{:S(2)}) collective-permute-start(bf16[128,2560]{1,0:T(8,128)(2,1)S(1)} %get-tuple-element.31), channel_id=1, source_target_pairs={{0,1},{1,0},{2,3},{3,2},{4,5},{5,4},{6,7},{7,6},{8,9},{9,8},{10,11... | collective-permute-start | bytes 1966088 | tf_op jit(solution)/shard_map/ppermute | solution.py:315
  86.2 16.0 %collective-permute-start.21 = (bf16[128,2560]{1,0:T(8,128)(2,1)S(1)}, bf16[128,2560]{1,0:T(8,128)(2,1)S(1)}, u32[]{:S(2)}, u32[]{:S(2)}) collective-permute-start(bf16[128,2560]{1,0:T(8,128)(2,1)S(1)} %add_convert_fusion.1), channel_id=1, source_target_pairs={{0,2},{1,3},{2,0},{3,1},{4,6},{5,7},{6,4},{7,5},{8,10},{9,11},{10,... | collective-permute-start | bytes 1966088 | tf_op jit(solution)/shard_map/ppermute | solution.py:315
  89.5 12.7 %collective-permute-start.20 = (bf16[128,2560]{1,0:T(8,128)(2,1)S(1)}, bf16[128,2560]{1,0:T(8,128)(2,1)S(1)}, u32[]{:S(2)}, u32[]{:S(2)}) collective-permute-start(bf16[128,2560]{1,0:T(8,128)(2,1)S(1)} %get-tuple-element.34), channel_id=1, source_target_pairs={{0,1},{1,0},{2,3},{3,2},{4,5},{5,4},{6,7},{7,6},{8,9},{9,8},{10,11... | collective-permute-start | bytes 1966088 | tf_op jit(solution)/shard_map/ppermute | solution.py:315
  (1 other events, 0.7 us)
